TPU v7x, 32 devices: a whole 2x2x4 slice. The times are simulated.
32 devices in a mesh: rows: 2 (over core), seq: 16 (over z, y, x).
Axes of the slice: x: 2, y: 2, z: 4, core: 2. Of those that a mesh axis runs over, the one named last changes fastest.
Arguments:
- tokens: bfloat16 [2, 2048, 2048], P('rows', 'seq'), may hold values from -6 to 6
- out_grad: bfloat16 [2, 2048, 2048], P('rows', 'seq'), may hold values from -6 to 6
- doc_lengths: int32 [2, 2], P('rows'), may hold values from 1 to 1536, 2048 in all within a row
- norm_attn: bfloat16 [2048], P(('rows', 'seq')), may hold values from 0.099609375 to 1.8984375
- w_qdown: bfloat16 [2048, 1024], P(('rows', 'seq')), may hold values from -0.125 to 0.125
- norm_query: bfloat16 [1024], P(('rows', 'seq')), may hold values from 0.099609375 to 1.8984375
- w_qup: bfloat16 [1024, 4096], P(('rows', 'seq')), may hold values from -0.1875 to 0.1875
- w_key: bfloat16 [2048, 256], P(('rows', 'seq')), may hold values from -0.125 to 0.125
- w_value: bfloat16 [2048, 256], P(('rows', 'seq')), may hold values from -0.125 to 0.125
- w_out: bfloat16 [4096, 2048], P(None, ('rows', 'seq')), may hold values from -0.375 to 0.375
- norm_ffn: bfloat16 [2048], P(('rows', 'seq')), may hold values from 0.099609375 to 1.8984375
- w_gate: bfloat16 [2048, 5632], P('rows', 'seq'), may hold values from -0.125 to 0.125
- w_up: bfloat16 [2048, 5632], P('rows', 'seq'), may hold values from -0.125 to 0.125
- w_down: bfloat16 [5632, 2048], P('seq', 'rows'), may hold values from -0.078125 to 0.078125
Outputs:
- output: bfloat16 [2, 2048, 2048], P('rows', 'seq')
- grad_tokens: bfloat16 [2, 2048, 2048], P('rows', 'seq')
- grad_norm_attn: float32 [2048], P(('rows', 'seq'))
- grad_w_qdown: float32 [2048, 1024], P(('rows', 'seq'))
- grad_norm_query: float32 [1024], P(('rows', 'seq'))
- grad_w_qup: float32 [1024, 4096], P(('rows', 'seq'))
- grad_w_key: float32 [2048, 256], P(('rows', 'seq'))
- grad_w_value: float32 [2048, 256], P(('rows', 'seq'))
- grad_w_out: float32 [4096, 2048], P(None, ('rows', 'seq'))
- grad_norm_ffn: float32 [2048], P(('rows', 'seq'))
- grad_w_gate: float32 [2048, 5632], P('rows', 'seq')
- grad_w_up: float32 [2048, 5632], P('rows', 'seq')
- grad_w_down: float32 [5632, 2048], P('seq', 'rows')
Inputs may be any that keep to these rules, and one draw needn't show every extreme that they name: `doc_lengths`: in each row the 2 document lengths add up to 2048; the longest document of every row has at most 1536 tokens.
All inputs are finite; a program needn't handle non-finite values.
Results may differ from a plain program's by a relative error of at most 0.02.
Values may be sent and summed in bfloat16 or wider, within the bound.
No kernel may reach another device: no remote copies, remote signals or barrier semaphores. Data moves between devices by JAX's collectives and lax.ppermute only.
A program may use at most 512 MiB of HBM per device.

v0:
```python
import jax
import jax.numpy as jnp
import numpy as np
from jax import lax
from jax.experimental import pallas as pl
from jax.experimental.pallas import tpu as pltpu
from jax.sharding import Mesh, PartitionSpec as P

HEADS = 16
HD = 256
PLANE = 4
EXTRA = 16

masked = -1e30
epsilon = 1e-05
BF = jnp.bfloat16
F32 = jnp.float32


def rms_norm(values, gain_vec):
    return (
        values * lax.rsqrt(jnp.mean(values * values, axis=-1, keepdims=True) + epsilon) * gain_vec
    )


def rope_tables(relative, half_dim):
    frequency = 1.0 / 10000.0 ** (jnp.arange(half_dim, dtype=F32) / half_dim)
    angles = relative.astype(F32)[..., None] * frequency
    return (jnp.cos(angles), jnp.sin(angles))


def doc_layout(lengths, positions):
    doc_ends = jnp.cumsum(lengths)
    passed = positions[:, None] >= doc_ends[None, :]
    segment = jnp.sum(passed.astype(jnp.int32), axis=1)
    doc_start = jnp.sum(jnp.where(passed, lengths[None, :], 0), axis=1)
    return (segment, positions - doc_start)


def mm(left, right):
    return jnp.dot(left, right, preferred_element_type=F32)


def mm_nt(left, right):
    return jnp.einsum("ik,jk->ij", left, right, preferred_element_type=F32)


def mm_tn(left, right):
    return jnp.einsum("ki,kj->ij", left, right, preferred_element_type=F32)


def shift(value, axis, by=1):
    count = lax.axis_size(axis)
    return lax.ppermute(value, axis, [(i, (i + by) % count) for i in range(count)])


def ring_gather(value, axis):
    pieces = [value]
    for _ in range(lax.axis_size(axis) - 1):
        pieces.append(shift(pieces[-1], axis))
    return pieces


def ring_spread(value, axis):
    return [value] + [shift(value, axis, k) for k in range(1, lax.axis_size(axis))]


def flip(value, by):
    if by == 3:
        return lax.ppermute(value, ("py", "px"), [(i, i ^ 3) for i in range(PLANE)])
    return lax.ppermute(value, "px" if by == 1 else "py", [(0, 1), (1, 0)])


def halves(value, axis=0):
    half = value.shape[axis] // 2
    return (
        lax.slice_in_dim(value, 0, half, axis=axis),
        lax.slice_in_dim(value, half, 2 * half, axis=axis),
    )


def plane_spread(value):
    return [value] + [flip(value, k) for k in range(1, PLANE)]


def plane_sum(parts):
    got = [flip(parts[k].astype(BF), k) for k in range(1, PLANE)]
    return sum((g.astype(F32) for g in got), parts[0].astype(F32))


def plane_swap(parts):
    return [parts[0]] + [flip(parts[k], k) for k in range(1, PLANE)]


def pick(stacked, index):
    return lax.dynamic_index_in_dim(stacked, index, 0, keepdims=False)


def place(items, count, unit=None, split=None):
    unit = unit or items[0][0].shape[0]
    columns = items[0][0].shape[1]
    pieces = [v.reshape(-1, unit, columns) for v, _ in items]
    number = len(pieces)
    cuts = [(0, unit)] if split is None else [(0, split), (split, unit)]

    def kernel(slots, *refs):
        outs, sems = refs[number:-1], refs[-1]
        copies = []
        for i in range(number):
            span = pl.ds(slots[i], pieces[i].shape[0])
            for j, (start, stop) in enumerate(cuts):
                source = refs[i] if split is None else refs[i].at[:, pl.ds(start, stop - start)]
                copies.append(pltpu.make_async_copy(source, outs[j].at[span], sems.at[i, j]))
        for copy in copies:
            copy.start()
        for copy in copies:
            copy.wait()

    shapes = [(count, stop - start, columns) for start, stop in cuts]
    outs = pl.pallas_call(
        kernel,
        grid_spec=pltpu.PrefetchScalarGridSpec(
            num_scalar_prefetch=1,
            grid=(1,),
            in_specs=[pl.BlockSpec(memory_space=pl.ANY)] * number,
            out_specs=[pl.BlockSpec(shape, lambda i, s: (0, 0, 0)) for shape in shapes],
            scratch_shapes=[pltpu.SemaphoreType.DMA((number, len(cuts)))],
        ),
        out_shape=[jax.ShapeDtypeStruct(shape, pieces[0].dtype) for shape in shapes],
        compiler_params=params(),
        cost_estimate=pl.CostEstimate(
            flops=0, bytes_accessed=4 * count * unit * columns, transcendentals=0
        ),
        name="place",
    )(jnp.stack([jnp.asarray(slot, jnp.int32) for _, slot in items]), *pieces)
    if split is None:
        return outs[0].reshape(-1, columns)
    return outs


def plane_place(blocks, index):
    return place([(p, index ^ k) for k, p in enumerate(blocks)], PLANE)


def ring_place(pieces, index):
    count = len(pieces)
    return place([(p, (index - k) % count) for k, p in enumerate(pieces)], count)


def block_of(value, index, size, axis=0):
    return lax.dynamic_slice_in_dim(value, index * size, size, axis)


def column_swap(weight, index):
    size = weight.shape[1] // PLANE
    parts = [block_of(weight, index ^ k, size, 1) for k in range(PLANE)]
    return place([(p, index ^ k) for k, p in enumerate(plane_swap(parts))], PLANE)


def rows_place(pieces, row, ring, split=None):
    rings, rows = len(pieces), lax.axis_size("rows")
    unit = pieces[0].shape[0] // PLANE
    own = ring_place(pieces, ring)
    items = [
        (got, (row - j) % rows * rings * PLANE) for j, got in enumerate(ring_spread(own, "rows"))
    ]
    return place(items, rings * rows * PLANE, unit, split)


def row_blocks(left, right, spot, extra=None):
    row, rows = spot[0], lax.axis_size("rows")
    size = left.shape[1] // rows

    def block(k):
        index = (row - k) % rows
        result = mm_tn(block_of(left, index, size, 1), right)
        if extra is not None:
            more = pick(extra, index)
            result = result.reshape(more.shape[0], -1, result.shape[1])
            result = jnp.concatenate([result, more], axis=1).reshape(-1, result.shape[2])
        return result

    return block


def over_rows(block):
    rows = lax.axis_size("rows")
    total = block(1).astype(BF) if rows > 1 else block(0)
    for k in range(2, rows + 1):
        total = shift(total, "rows").astype(F32) + block(k % rows)
        total = total.astype(BF)
    return total


def ring_parts(total, spot):
    ring, rings = spot[1], lax.axis_size("ring")
    size = total.shape[0] // rings
    return [block_of(total, (ring - k) % rings, size) for k in range(rings)]


def over_plane(total, spot, split):
    plane = spot[2]
    size = total.shape[0] // PLANE
    got = plane_swap([block_of(total, plane ^ k, size) for k in range(PLANE)])
    return place([(g, plane ^ k) for k, g in enumerate(got)], PLANE, None, split)


def ring_steps(parts, first, last, total=None):
    count = len(parts)
    total = parts[1] if total is None else total
    for k in range(first + 1, last + 2):
        total = shift(total, "ring").astype(F32) + parts[k % count].astype(F32)
        if k < count:
            total = total.astype(BF)
    return total


def tie(value, *deps):
    return lax.optimization_barrier((value,) + deps)


def params():
    return pltpu.CompilerParams(vmem_limit_bytes=56 * 1024 * 1024)


def dot_nn(left, right):
    return lax.dot_general(left, right, (((1,), (0,)), ((), ())), preferred_element_type=F32)


def dot_nt(left, right):
    return lax.dot_general(left, right, (((1,), (1,)), ((), ())), preferred_element_type=F32)


def dot_tn(left, right):
    return lax.dot_general(left, right, (((0,), (0,)), ((), ())), preferred_element_type=F32)


QB = 256
KB = 512
HALF = HD // 2


def query_bounds(scal, ndoc, block):
    first = scal[1] + block * QB
    positions = first + lax.broadcasted_iota(jnp.int32, (QB, 1), 0)
    starts = jnp.zeros((QB, 1), jnp.int32)
    low_start, end = 0, 0
    for n in range(ndoc):
        end = end + scal[2 + n]
        starts = jnp.where(positions >= end, end, starts)
        low_start = jnp.where(first >= end, end, low_start)
    return positions, starts, lax.div(low_start, KB), lax.div(first + QB - 1, KB) + 1


def attend_kernel(ndoc, scal, q_raw, p0, p1, p2, p3, cos, sin, att, q_out, lse, keys, values):
    block = pl.program_id(0)
    heads = q_raw.shape[1] // HD

    @pl.when(block == 0)
    def _():
        plane = scal[0]
        for i in range(PLANE):
            dest = keys if i < 2 else values
            side = slice((i % 2) * HALF, (i % 2 + 1) * HALF)
            for j, piece in enumerate((p0, p1, p2, p3)):

                @pl.when(plane == (i ^ j))
                def _(dest=dest, side=side, piece=piece):
                    dest[:, side] = piece[...]

        front, back = keys[:, :HALF].astype(F32), keys[:, HALF:].astype(F32)
        keys[:, :HALF] = (front * cos[...] - back * sin[...]).astype(BF)
        keys[:, HALF:] = (back * cos[...] + front * sin[...]).astype(BF)

    rows = pl.ds(pl.multiple_of(scal[1] + block * QB, QB), QB)
    q_cos, q_sin = cos[rows, :], sin[rows, :]
    for h in range(heads):
        front = q_raw[:, h * HD : h * HD + HALF]
        back = q_raw[:, h * HD + HALF : (h + 1) * HD]
        query = jnp.concatenate(
            [front * q_cos - back * q_sin, back * q_cos + front * q_sin], axis=1
        ).astype(BF)
        q_out[:, h * HD : (h + 1) * HD] = query * jnp.asarray(HD**-0.5, BF)
    positions, starts, low, high = query_bounds(scal, ndoc, block)

    def step(kb, carry):
        span = pl.ds(pl.multiple_of(kb * KB, KB), KB)
        where = kb * KB + lax.broadcasted_iota(jnp.int32, (QB, KB), 1)
        allowed = (where <= positions) & (where >= starts)
        key, value = keys[span, :], values[span, :]
        result = []
        for h in range(heads):
            peak, total, mixed = carry[h]
            scores = dot_nt(q_out[:, h * HD : (h + 1) * HD], key)
            scores = jnp.where(allowed, scores, masked)
            new_peak = jnp.maximum(peak, jnp.max(scores, axis=1, keepdims=True))
            weights = jnp.exp(scores - new_peak)
            keep = jnp.exp(peak - new_peak)
            total = total * keep + jnp.sum(weights, axis=1, keepdims=True)
            mixed = mixed * keep + dot_nn(weights.astype(BF), value)
            result.append((new_peak, total, mixed))
        return tuple(result)

    first = (jnp.full((QB, 1), -3e38, F32), jnp.zeros((QB, 1), F32), jnp.zeros((QB, HD), F32))
    done = lax.fori_loop(low, high, step, (first,) * heads)
    for h, (peak, total, mixed) in enumerate(done):
        att[:, h * HD : (h + 1) * HD] = (mixed / total).astype(BF)
        lse[:, h * 128 : (h + 1) * 128] = jnp.broadcast_to(peak + jnp.log(total), (QB, 128))


def attend(scal, query_raw, pieces, cos, sin):
    group, wide = query_raw.shape
    length = cos.shape[0]
    heads = wide // HD
    whole = pl.BlockSpec((length, HALF), lambda i, s: (0, 0))
    token = pl.BlockSpec((QB, wide), lambda i, s: (i, 0))
    return pl.pallas_call(
        lambda *refs: attend_kernel(scal.shape[0] - 2, *refs),
        grid_spec=pltpu.PrefetchScalarGridSpec(
            num_scalar_prefetch=1,
            grid=(group // QB,),
            in_specs=[token] + [whole] * 6,
            out_specs=[
                token,
                token,
                pl.BlockSpec((QB, heads * 128), lambda i, s: (i, 0)),
                pl.BlockSpec((length, HD), lambda i, s: (0, 0)),
                pl.BlockSpec((length, HD), lambda i, s: (0, 0)),
            ],
        ),
        out_shape=[
            jax.ShapeDtypeStruct((group, wide), BF),
            jax.ShapeDtypeStruct((group, wide), BF),
            jax.ShapeDtypeStruct((group, heads * 128), F32),
            jax.ShapeDtypeStruct((length, HD), BF),
            jax.ShapeDtypeStruct((length, HD), BF),
        ],
        compiler_params=params(),
        cost_estimate=pl.CostEstimate(
            flops=4 * group * wide * length, bytes_accessed=8 << 20, transcendentals=0
        ),
        name="attend",
    )(scal, query_raw, *pieces, cos, sin)


def attend_back_kernel(
    ndoc, scal, query, keys, values, lse, att, d_att, cos, sin, dep, d_raw, parts, d_keys, d_values
):
    block = pl.program_id(0)
    heads = query.shape[1] // HD

    @pl.when(block == 0)
    def _():
        d_keys[...] = jnp.zeros_like(d_keys)
        d_values[...] = jnp.zeros_like(d_values)

    positions, starts, low, high = query_bounds(scal, ndoc, block)
    spans = [slice(h * HD, (h + 1) * HD) for h in range(heads)]
    shared = [
        jnp.sum(d_att[:, s].astype(F32) * att[:, s].astype(F32), axis=1, keepdims=True)
        for s in spans
    ]

    def step(kb, d_queries):
        span = pl.ds(pl.multiple_of(kb * KB, KB), KB)
        key, value = keys[span, :], values[span, :]
        where = kb * KB + lax.broadcasted_iota(jnp.int32, (QB, KB), 1)
        allowed = (where <= positions) & (where >= starts)
        result = []
        d_key, d_value = d_keys[span, :], d_values[span, :]
        for h in range(heads):
            scores = dot_nt(query[:, spans[h]], key)
            scores = jnp.where(allowed, scores, masked)
            probs = jnp.exp(scores - lse[:, h * 128 : h * 128 + 1])
            d_probs = dot_nt(d_att[:, spans[h]], value)
            d_scores = (probs * (d_probs - shared[h])).astype(BF)
            d_key = d_key + dot_tn(d_scores, query[:, spans[h]])
            d_value = d_value + dot_tn(probs.astype(BF), d_att[:, spans[h]])
            result.append(d_queries[h] + dot_nn(d_scores, key))
        d_keys[span, :] = d_key
        d_values[span, :] = d_value
        return tuple(result)

    done = lax.fori_loop(low, high, step, (jnp.zeros((QB, HD), F32),) * heads)
    rows = pl.ds(pl.multiple_of(scal[1] + block * QB, QB), QB)
    q_cos, q_sin = cos[rows, :], sin[rows, :]
    for h, d_query in enumerate(done):
        d_query = d_query * HD**-0.5
        front, back = d_query[:, :HALF], d_query[:, HALF:]
        d_raw[:, h * HD : h * HD + HALF] = (front * q_cos + back * q_sin).astype(BF)
        d_raw[:, h * HD + HALF : (h + 1) * HD] = (back * q_cos - front * q_sin).astype(BF)

    @pl.when(block == pl.num_programs(0) - 1)
    def _():
        plane = scal[0]
        front, back = d_keys[:, :HALF], d_keys[:, HALF:]
        parts[plane] = (front * cos[...] + back * sin[...]).astype(BF)
        parts[plane ^ 1] = (back * cos[...] - front * sin[...]).astype(BF)
        parts[plane ^ 2] = d_values[:, :HALF].astype(BF)
        parts[plane ^ 3] = d_values[:, HALF:].astype(BF)


def attend_back(scal, query, keys, values, lse, att, d_att, cos, sin, dep):
    group, wide = query.shape
    length = cos.shape[0]
    heads = wide // HD
    token = pl.BlockSpec((QB, wide), lambda i, s: (i, 0))
    table = pl.BlockSpec((length, HALF), lambda i, s: (0, 0))
    whole = pl.BlockSpec((length, HD), lambda i, s: (0, 0))
    return pl.pallas_call(
        lambda *refs: attend_back_kernel(scal.shape[0] - 2, *refs),
        grid_spec=pltpu.PrefetchScalarGridSpec(
            num_scalar_prefetch=1,
            grid=(group // QB,),
            in_specs=[token, whole, whole, pl.BlockSpec((QB, heads * 128), lambda i, s: (i, 0))]
            + [token, token, table, table, pl.BlockSpec(memory_space=pl.ANY)],
            out_specs=[token, pl.BlockSpec((PLANE, length, HALF), lambda i, s: (0, 0, 0))],
            scratch_shapes=[pltpu.VMEM((length, HD), F32), pltpu.VMEM((length, HD), F32)],
        ),
        out_shape=[
            jax.ShapeDtypeStruct((group, wide), BF),
            jax.ShapeDtypeStruct((PLANE, length, HALF), BF),
        ],
        compiler_params=params(),
        cost_estimate=pl.CostEstimate(
            flops=10 * group * wide * length, bytes_accessed=12 << 20, transcendentals=0
        ),
        name="attend_back",
    )(scal, query, keys, values, lse, att, d_att, cos, sin, dep)


def ffn_kernel(chunk, count, blocks, slots, *refs):
    h_refs, dy_ref, w_ref, refs = refs[:count], refs[count], refs[count + 1], refs[count + 2 :]
    if chunk:
        refs = refs[3:]
    acts, h_all, dy_all = refs[:3]
    d_h, out = refs[3 : 3 + count], refs[3 + count : 3 + 2 * count]
    gate_up, down, sems, dy_sems = refs[3 + 2 * count :]
    units = down.shape[1]
    own = units // PLANE
    rows = h_refs[0].shape[0]
    copies = []
    for block in range(blocks):
        for k in range(PLANE):
            at = block * PLANE + k
            for part in range(3):
                source = w_ref.at[pl.ds((3 * at + part) * own, own)]
                if part < 2:
                    dest = gate_up.at[block, pl.ds(part * units + k * own, own)]
                else:
                    dest = down.at[block, pl.ds(k * own, own)]
                copies.append((part, pltpu.make_async_copy(source, dest, sems.at[at, part])))
    for k in range(count):
        source = dy_ref.at[pl.ds(pl.multiple_of(slots[k] * rows, rows), rows)]
        dest = dy_all.at[pl.ds(k * rows, rows)]
        copies.insert(0, (2, pltpu.make_async_copy(source, dest, dy_sems.at[k])))
    for part in range(3):
        for kind, copy in copies:
            if kind == part:
                copy.start()
    for k in range(count):
        h_all[k * rows : (k + 1) * rows, :] = h_refs[k][...]
    feat = h_all.shape[1] // blocks

    def cols(ref, k):
        return ref[:, k * feat : (k + 1) * feat]

    def wait(part):
        for kind, copy in copies:
            if kind == part:
                copy.wait()

    wait(0)
    gate = sum(dot_nt(cols(h_all, k), gate_up[k, :units, :]) for k in range(blocks))
    wait(1)
    up = sum(dot_nt(cols(h_all, k), gate_up[k, units:, :]) for k in range(blocks))
    sig = 1.0 / (1.0 + jnp.exp(-gate))
    silu = gate * sig
    hid = (silu * up).astype(BF)
    acts[2] = hid
    wait(2)
    d_hidden = sum(dot_nt(cols(dy_all, k), down[k]) for k in range(blocks))
    d_gate = (d_hidden * up * (sig + silu * (1.0 - sig))).astype(BF)
    d_up = (d_hidden * silu).astype(BF)
    acts[0] = d_gate
    acts[1] = d_up
    for k in range(blocks):
        span = slice(k * feat, (k + 1) * feat)
        grad = dot_nn(d_gate, gate_up[k, :units, :]) + dot_nn(d_up, gate_up[k, units:, :])
        result = dot_nn(hid, down[k])
        for j in range(count):
            d_h[j][:, span] = grad[j * rows : (j + 1) * rows].astype(BF)
            out[j][:, span] = result[j * rows : (j + 1) * rows].astype(BF)


def feed_forward(chunk, chunks, slots, h, dy, weights, held):
    count = len(h)
    rows, width = h[0].shape
    feat = weights.shape[1]
    blocks = width // feat
    units = weights.shape[0] // blocks // 3
    total = rows * count
    whole = pl.BlockSpec((rows, width), lambda i, s: (0, 0))
    anywhere = pl.BlockSpec(memory_space=pl.ANY)
    return pl.pallas_call(
        lambda *refs: ffn_kernel(chunk, count, blocks, *refs),
        grid_spec=pltpu.PrefetchScalarGridSpec(
            num_scalar_prefetch=1,
            grid=(1,),
            in_specs=[whole] * count + [anywhere] * (2 + len(held)),
            out_specs=[pl.BlockSpec((3, total, units), lambda i, s: (0, chunk, 0))]
            + [pl.BlockSpec((total, width), lambda i, s: (chunk, 0))] * 2
            + [whole] * (2 * count),
            scratch_shapes=[
                pltpu.VMEM((blocks, 2 * units, feat), BF),
                pltpu.VMEM((blocks, units, feat), BF),
                pltpu.SemaphoreType.DMA((blocks * PLANE, 3)),
                pltpu.SemaphoreType.DMA((count,)),
            ],
        ),
        out_shape=[jax.ShapeDtypeStruct((3, total * chunks, units), BF)]
        + [jax.ShapeDtypeStruct((total * chunks, width), BF)] * 2
        + [jax.ShapeDtypeStruct((rows, width), BF)] * (2 * count),
        input_output_aliases={3 + count + i: i for i in range(len(held))},
        compiler_params=params(),
        cost_estimate=pl.CostEstimate(
            flops=12 * total * width * units, bytes_accessed=24 << 20, transcendentals=0
        ),
        name="feed_forward",
    )(slots, *h, dy, weights, *held)


def ffn_gradient(acts, h, dy, blocks):
    count, width = h.shape
    units = acts.shape[2]
    feat = width // blocks

    def kernel(left, h_ref, dy_ref, out):
        def store(right):
            result = dot_tn(left[0], right).astype(BF)
            for k in range(PLANE):
                out[0, k, 0] = result[k * (units // PLANE) : (k + 1) * (units // PLANE)]

        part = pl.program_id(1)

        @pl.when(part < 2)
        def _():
            store(h_ref[...])

        @pl.when(part == 2)
        def _():
            store(dy_ref[...])

    right = pl.BlockSpec((count, feat), lambda k, part: (0, k))
    out = pl.pallas_call(
        kernel,
        grid=(blocks, 3),
        in_specs=[pl.BlockSpec((1, count, units), lambda k, part: (part, 0, 0)), right, right],
        out_specs=pl.BlockSpec(
            (1, PLANE, 1, units // PLANE, feat), lambda k, part: (k, 0, part, 0, 0)
        ),
        out_shape=jax.ShapeDtypeStruct((blocks, PLANE, 3, units // PLANE, feat), BF),
        compiler_params=params(),
        cost_estimate=pl.CostEstimate(
            flops=6 * count * width * units, bytes_accessed=24 << 20, transcendentals=0
        ),
        name="ffn_gradient",
    )(acts, h, dy)
    return out.reshape(-1, feat)


def shards(
    tokens,
    out_grad,
    doc_lengths,
    norm_attn,
    w_qdown,
    norm_query,
    w_qup,
    w_key,
    w_value,
    w_out,
    norm_ffn,
    w_gate,
    w_up,
    w_down,
):
    rows, rings = lax.axis_size("rows"), lax.axis_size("ring")
    devices = rows * rings * PLANE
    row = lax.axis_index("rows")
    ring = lax.axis_index("ring")
    plane = lax.axis_index("py") * 2 + lax.axis_index("px")
    spot = (row, ring, plane)
    own_tokens = tokens[0]
    count_local, width = own_tokens.shape
    group = count_local * PLANE
    row_length = group * rings

    latent_width = w_qdown.shape[1] // PLANE
    kv_width = 2 * HD // PLANE
    kv_w = jnp.concatenate([w_key, w_value], axis=1)
    down_w = jnp.concatenate(
        [
            piece
            for i in range(PLANE)
            for piece in (
                w_qdown[:, i * latent_width : (i + 1) * latent_width],
                kv_w[:, i * kv_width : (i + 1) * kv_width],
            )
        ],
        axis=1,
    )
    part_a, part_q = norm_attn.shape[0], norm_query.shape[0]
    gains = jnp.concatenate([norm_attn, norm_query, norm_ffn])
    gain_count = gains.shape[0]
    lanes = latent_width + kv_width
    gains = jnp.tile(jnp.pad(gains, (0, lanes - gain_count)), PLANE)
    gains = jnp.pad(gains[None], ((0, EXTRA - 1), (0, 0)))
    block_rows = down_w.shape[0]
    hidden_axes = ("rows", "py", "px")
    down_w = column_swap(jnp.concatenate([down_w, gains]), plane)
    ffn_w = jnp.concatenate([jnp.transpose(w_gate), jnp.transpose(w_up), w_down])
    token_blocks = plane_spread(own_tokens)
    ffn_w = lax.all_gather(ffn_w, hidden_axes, axis=0, tiled=True)
    down_ring = ring_spread(down_w, "ring")
    other_w = jnp.concatenate([w_qup, jnp.transpose(w_out)])
    other_w = column_swap(other_w, plane)
    other_w = other_w.reshape(PLANE, -1, other_w.shape[1])
    up_rows = w_qup.shape[0]
    up_query = other_w[:, :up_rows].reshape(-1, other_w.shape[2])
    out_proj = other_w[:, up_rows:].reshape(-1, other_w.shape[2])
    up_query, *down_ring = tie(up_query, *down_ring)
    down_fin, gains = rows_place(down_ring, row, ring, block_rows)
    up_ring = ring_gather(up_query, "ring")
    out_proj, *up_ring = tie(out_proj, *up_ring)
    out_proj = rows_place(ring_gather(out_proj, "ring"), row, ring)
    upstream = out_grad[0]
    ring_upstream = upstream
    ring_upstream, ffn_w = tie(upstream, ffn_w)
    ring_upstream = lax.all_gather(ring_upstream, "ring", axis=0, tiled=True)
    down_w = down_fin.reshape(-1, lanes)
    gains = gains[:, 0, :gain_count].astype(F32)
    gain_attn = gains[:, :part_a].reshape(-1)
    gain_query = gains[:, part_a : part_a + part_q].reshape(-1)
    gain_ffn = gains[:, part_a + part_q :].reshape(-1)

    key_positions = jnp.arange(row_length, dtype=jnp.int32)
    key_relative = doc_layout(doc_lengths[0], key_positions)[1]
    key_cos, key_sin = rope_tables(key_relative, HD // 2)
    scal = jnp.concatenate([jnp.stack([plane, ring * group]), doc_lengths[0]]).astype(jnp.int32)

    group_tokens = plane_place(token_blocks, plane).astype(F32)
    normed = rms_norm(group_tokens, gain_attn).astype(BF)
    projected = mm(normed, down_w).astype(BF)

    up_query = rows_place(up_ring, row, ring)
    key_value = ring_spread(projected[:, latent_width:], "ring")
    latent = plane_spread(projected[:, :latent_width])
    key_value = ring_place(key_value, ring)
    key_value, *latent = tie(key_value, *latent)
    latent = jnp.stack(latent)
    latent = jnp.concatenate([pick(latent, plane ^ i) for i in range(PLANE)], axis=1).astype(F32)
    latent_normed = rms_norm(latent, gain_query).astype(BF)
    query_raw = mm(latent_normed, up_query)

    key_value = plane_spread(key_value)
    query_raw, out_proj = tie(query_raw, out_proj)
    attended, queries, log_total, all_keys, all_values = attend(
        scal, query_raw, key_value, key_cos, key_sin
    )
    branch = mm_nt(attended, out_proj)
    branch = plane_sum([block_of(branch, plane ^ k, count_local) for k in range(PLANE)])
    middle = own_tokens.astype(F32) + branch

    normed2_f, pull_ffn_norm = jax.vjp(rms_norm, middle, gain_ffn)
    normed_ffn = normed2_f.astype(BF)
    chunk = 2
    chunks = rings // chunk
    held = []
    grad_parts, out_parts = [], []
    ring_normed = [normed_ffn]
    for k in range(1, rings):
        last = ring_normed[-1]
        if k > 1 and k % chunk == chunk - 1:
            last, *held = tie(last, *held)
        ring_normed.append(shift(last, "ring"))
        if k % chunk != chunk - 1:
            continue
        some = slice(k - chunk + 1, k + 1)
        slots = (ring - jnp.arange(k - chunk + 1, k + 1)) % rings
        results = feed_forward(
            k // chunk, chunks, slots, ring_normed[some], ring_upstream, ffn_w, held
        )
        held = results[:3]
        grad_parts += results[3 : 3 + chunk]
        out_parts += results[3 + chunk :]
    grad_normed_ffn = ring_steps(grad_parts, 1, rings - 2)
    ffn_grad, grad_normed_ffn = tie(ffn_gradient(*held, rows), grad_normed_ffn)
    ffn_grad = lax.psum_scatter(ffn_grad, hidden_axes, scatter_dimension=0, tiled=True)
    grad_normed_ffn = ring_steps(grad_parts, rings - 1, rings - 1, grad_normed_ffn)
    grad_normed_ffn, *out_parts = tie(grad_normed_ffn, *out_parts)
    out_total = ring_steps(out_parts, 1, rings - 2)
    output = ring_steps(out_parts, rings - 1, rings - 1, out_total)

    upstream_f = upstream.astype(F32)
    grad_middle_norm, grad_gain_ffn = pull_ffn_norm(grad_normed_ffn)
    grad_middle = upstream_f + grad_middle_norm

    branch_grad = grad_middle.astype(BF)
    branch_blocks = plane_spread(branch_grad)
    branch_grad = plane_place(branch_blocks, plane)
    grad_attended = mm(branch_grad, out_proj).astype(BF)
    grad_query_raw, kv_parts = attend_back(
        scal,
        queries,
        all_keys,
        all_values,
        log_total,
        attended,
        grad_attended,
        key_cos,
        key_sin,
        out_total,
    )
    grad_out_w = over_rows(row_blocks(branch_grad, attended, spot))
    grad_out_w, output = tie(grad_out_w, output)
    output = middle + output
    grad_up_query = over_rows(row_blocks(latent_normed, grad_query_raw, spot))
    both = [g.reshape(rings * PLANE, -1, g.shape[1]) for g in (grad_up_query, grad_out_w)]
    wide_parts = jnp.concatenate(both, axis=1).reshape(-1, grad_out_w.shape[1])
    wide_parts = ring_parts(wide_parts, spot)
    wide_grad = ring_steps(wide_parts, 1, 1)
    grad_latent_normed = mm_nt(grad_query_raw, up_query)
    kv_grad = plane_sum([kv_parts[k] for k in range(PLANE)]).astype(BF)
    kv_grad, grad_latent_normed = tie(kv_grad, grad_latent_normed)
    kv_grad, wide_grad = tie(kv_grad, wide_grad)
    kv_grad = ring_steps(
        [block_of(kv_grad, (ring - k) % rings, group) for k in range(rings)], 1, rings - 1
    )
    wide_grad = ring_steps(wide_parts, 2, rings - 1, wide_grad).astype(BF)
    grad_latent_normed = plane_sum(
        [block_of(grad_latent_normed, plane ^ k, count_local) for k in range(PLANE)]
    )
    own_latent = block_of(latent, plane, count_local)
    pull_latent = jax.vjp(rms_norm, own_latent, gain_query)[1]
    grad_latent, grad_gain_query = pull_latent(grad_latent_normed)
    grad_latent = grad_latent.astype(BF)
    grad_latent = plane_swap(
        [block_of(grad_latent, plane ^ k, latent_width, 1) for k in range(PLANE)]
    )
    grad_latent = place([(g, plane ^ k) for k, g in enumerate(grad_latent)], PLANE)
    grad_projected = jnp.concatenate([grad_latent, kv_grad.astype(BF)], axis=1)
    grad_projected, wide_grad = tie(grad_projected, wide_grad)
    grad_normed = mm_nt(grad_projected, down_w)
    pull_attn_norm = jax.vjp(rms_norm, own_tokens.astype(F32), gain_attn)[1]
    scale = lax.rsqrt(jnp.mean(group_tokens * group_tokens, axis=-1, keepdims=True) + epsilon)
    grad_gain_attn = jnp.sum(grad_normed * group_tokens * scale, axis=0)
    gain_grads = jnp.concatenate(
        [g.reshape(devices, -1) for g in (grad_gain_attn, grad_gain_query, grad_gain_ffn)], axis=1
    )
    gain_grads = jnp.pad(gain_grads[:, None], ((0, 0), (0, EXTRA - 1), (0, lanes - gain_count)))
    gain_grads = gain_grads.reshape(rows, rings * PLANE, EXTRA, lanes)
    grad_down = over_rows(row_blocks(normed, grad_projected, spot, gain_grads))
    down_parts = ring_parts(grad_down, spot)
    ffn_grad = ffn_grad.astype(F32).reshape(3, -1, ffn_grad.shape[1])
    gate_grad, up_grad, down_grad = jnp.transpose(ffn_grad[0]), jnp.transpose(ffn_grad[1]), ffn_grad[2]
    grad_down = ring_steps(down_parts, 1, 1)
    grad_down, grad_normed = tie(grad_down, grad_normed)
    grad_down = ring_steps(down_parts, 2, rings - 1, grad_down)
    grad_down = grad_down.astype(BF)
    grad_up_query, grad_out_w = over_plane(wide_grad, spot, up_rows)
    grad_up_query = jnp.concatenate(list(grad_up_query), axis=1).astype(F32)
    grad_out_w = jnp.transpose(jnp.concatenate(list(grad_out_w), axis=1).astype(F32))
    grad_normed = plane_sum(
        [block_of(grad_normed, plane ^ k, count_local) for k in range(PLANE)]
    )
    grad_input = grad_middle + pull_attn_norm(grad_normed)[0]
    size = grad_down.shape[0] // PLANE
    grad_down = plane_swap([block_of(grad_down, plane ^ k, size) for k in range(PLANE)])
    grad_gains = sum(g[block_rows, :gain_count].astype(F32) for g in grad_down)
    grad_down = jnp.stack([g[:block_rows] for g in grad_down])
    grad_down = [pick(grad_down, plane ^ i).astype(F32) for i in range(PLANE)]
    grad_down_query = jnp.concatenate([p[:, :latent_width] for p in grad_down], axis=1)
    grad_kv_w = jnp.concatenate([p[:, latent_width:] for p in grad_down], axis=1)

    return (
        output.astype(BF)[None],
        grad_input.astype(BF)[None],
        grad_gains[:part_a],
        grad_down_query,
        grad_gains[part_a : part_a + part_q],
        grad_up_query,
        grad_kv_w[:, :HD],
        grad_kv_w[:, HD:],
        grad_out_w,
        grad_gains[part_a + part_q :],
        gate_grad,
        up_grad,
        down_grad,
    )


def solution(mesh):
    rows = mesh.shape["rows"]
    chips = mesh.shape["seq"]
    inner = Mesh(
        np.asarray(mesh.devices).reshape(rows, chips // PLANE, 2, 2), ("rows", "ring", "py", "px")
    )
    seq = ("ring", "py", "px")
    every = ("rows",) + seq
    placed = (
        P("rows", seq, None),
        P("rows", seq, None),
        P("rows", None),
        P(every),
        P(every, None),
        P(every),
        P(every, None),
        P(every, None),
        P(every, None),
        P(None, every),
        P(every),
        P("rows", seq),
        P("rows", seq),
        P(seq, "rows"),
    )
    return jax.shard_map(
        shards,
        mesh=inner,
        in_specs=placed,
        out_specs=(
            P("rows", seq, None),
            P("rows", seq, None),
            P(every),
            P(every, None),
            P(every),
            P(every, None),
            P(every, None),
            P(every, None),
            P(None, every),
            P(every),
            P("rows", seq),
            P("rows", seq),
            P(seq, "rows"),
        ),
        check_vma=False,
    )
```

profile of v0, /device:TPU:0, one launch (start us, length us, event | category | flops | bytes accessed | tf_op | source)
XLA Modules:
  0.0 565.1 jit_solution(12019137141677886788)
XLA Ops:
  34.4 11.7 %collective-permute-done.4 = bf16[96,1024]{1,0:T(8,128)(2,1)S(1)} collective-permute-done((bf16[96,1024]{1,0:T(8,128)(2,1)S(1)}, bf16[96,1024]{1,0:T(8,128)(2,1)S(1)}, u32[]{:S(2)}, u32[]{:S(2)}) %collective-permute-start.4) | collective-permute-done | bytes 196640 | tf_op jit(solution)/shard_map/ppermute | solution.py:71
  61.0 9.3 %collective-permute-done.20 = bf16[128,1024]{1,0:T(8,128)(2,1)} collective-permute-done((bf16[128,1024]{1,0:T(8,128)(2,1)S(1)}, bf16[128,1024]{1,0:T(8,128)(2,1)}, u32[]{:S(2)}, u32[]{:S(2)}) %collective-permute-start.20) | collective-permute-done | bytes 262176 | tf_op jit(solution)/shard_map/ppermute | solution.py:54
  71.0 12.8 %collective-permute-done.1 = bf16[128,2048]{1,0:T(8,128)(2,1)S(1)} collective-permute-done((bf16[128,2048]{1,0:T(8,128)(2,1)S(1)}, bf16[128,2048]{1,0:T(8,128)(2,1)S(1)}, u32[]{:S(2)}, u32[]{:S(2)}) %collective-permute-start.1) | collective-permute-done | bytes 524320 | tf_op jit(solution)/shard_map/ppermute | solution.py:71
  98.3 5.1 collective-permute-done.23
  105.7 10.7 %collective-permute-done.24 = bf16[256,1024]{1,0:T(8,128)(2,1)S(1)} collective-permute-done((bf16[256,1024]{1,0:T(8,128)(2,1)S(1)}, bf16[256,1024]{1,0:T(8,128)(2,1)S(1)}, u32[]{:S(2)}, u32[]{:S(2)}) %collective-permute-start.24) | collective-permute-done | bytes 524320 | tf_op jit(solution)/shard_map/ppermute | solution.py:54
  124.4 5.5 collective-permute-done.25
  142.8 5.5 multiply_sine_fusion
  166.8 5.0 place.22
  172.1 8.3 %collective-permute-done.28.refs_4_ = bf16[2048,128]{1,0:T(8,128)(2,1)} collective-permute-done((bf16[2048,128]{1,0:T(8,128)(2,1)}, bf16[2048,128]{1,0:T(8,128)(2,1)}, u32[]{:S(2)}, u32[]{:S(2)}) %collective-permute-start.28) | collective-permute-done | bytes 524320 | tf_op jit(solution)/shard_map/ppermute | solution.py:71
  180.4 10.8 %attend.1 = (bf16[512,1024]{1,0:T(8,128)(2,1)}, bf16[512,1024]{1,0:T(8,128)(2,1)}, f32[512,512]{1,0:T(8,128)}, bf16[2048,256]{1,0:T(8,128)(2,1)}, bf16[2048,256]{1,0:T(8,128)(2,1)}) custom-call(s32[4]{0:T(128)} %pad_add_fusion.refs_0_, f32[512,1024]{1,0:T(8,128)} %fusion.65.refs_1_, bf16[2048,128]{1,0:T(8,128)(2,1)} %bitcast.275, ...), custom_call_target="tpu_custom_call" | custom-call | flops 4294967296 | bytes 8388608 | tf_op jit(solution)/shard_map/attend/pallas_call | solution.py:317
  201.6 11.5 %collective-permute-done.30 = bf16[128,2048]{1,0:T(8,128)(2,1)S(1)} collective-permute-done((bf16[128,2048]{1,0:T(8,128)(2,1)}, bf16[128,2048]{1,0:T(8,128)(2,1)S(1)}, u32[]{:S(2)}, u32[]{:S(2)}) %collective-permute-start.30) | collective-permute-done | bytes 524320 | tf_op jit(solution)/shard_map/ppermute | solution.py:71
  213.1 8.8 %collective-permute-done.31 = bf16[128,2048]{1,0:T(8,128)(2,1)S(1)} collective-permute-done((bf16[128,2048]{1,0:T(8,128)(2,1)}, bf16[128,2048]{1,0:T(8,128)(2,1)S(1)}, u32[]{:S(2)}, u32[]{:S(2)}) %collective-permute-start.31) | collective-permute-done | bytes 524320 | tf_op jit(solution)/shard_map/ppermute | solution.py:71
  229.3 8.8 %collective-permute-done.33.refs_2_ = bf16[128,2048]{1,0:T(8,128)(2,1)} collective-permute-done((bf16[128,2048]{1,0:T(8,128)(2,1)S(1)}, bf16[128,2048]{1,0:T(8,128)(2,1)}, u32[]{:S(2)}, u32[]{:S(2)}) %collective-permute-start.33) | collective-permute-done | bytes 524320 | tf_op jit(solution)/shard_map/ppermute | solution.py:54
  240.7 18.0 %feed_forward.2 = (bf16[3,512,1408]{2,1,0:T(8,128)(2,1)}, bf16[512,2048]{1,0:T(8,128)(2,1)}, bf16[512,2048]{1,0:T(8,128)(2,1)}, bf16[128,2048]{1,0:T(8,128)(2,1)...) custom-call(s32[2]{0:T(128)} %and_select_fusion.refs_0_, ...), custom_call_target="tpu_custom_call" | custom-call | flops 8858370048 | bytes 25165824 | tf_op jit(solution)/shard_map/feed_forward/pallas_call | solution.py:505
  261.2 13.5 %collective-permute-done.35.refs_2_ = bf16[128,2048]{1,0:T(8,128)(2,1)S(1)} collective-permute-done((bf16[128,2048]{1,0:T(8,128)(2,1)}, bf16[128,2048]{1,0:T(8,128)(2,1)S(1)}, u32[]{:S(2)}, u32[]{:S(2)}) %collective-permute-start.35) | collective-permute-done | bytes 524320 | tf_op jit(solution)/shard_map/ppermute | solution.py:54
  275.4 18.0 %feed_forward.3 = (bf16[3,512,1408]{2,1,0:T(8,128)(2,1)}, bf16[512,2048]{1,0:T(8,128)(2,1)}, bf16[512,2048]{1,0:T(8,128)(2,1)}, bf16[128,2048]{1,0:T(8,128)(2,1)...) custom-call(s32[2]{0:T(128)} %and_select_fusion.1.refs_0_, ...), custom_call_target="tpu_custom_call", output_to_operand_aliasing={{0}: (5, {}), {1}: (6, {}), {2}: (7, {})} | custom-call | flops 8858370048 | bytes 25165824 | tf_op jit(solution)/shard_map/feed_forward/pallas_call | solution.py:505
  294.7 16.0 %ffn_gradient.1 = bf16[2,4,3,352,1024]{4,3,2,1,0:T(8,128)(2,1)} custom-call(bf16[3,512,1408]{2,1,0:T(8,128)(2,1)} %get-tuple-element.107.left, bf16[512,2048]{1,0:T(8,128)(2,1)} %get-tuple-element.108.h_ref, bf16[512,2048]{1,0:T(8,128)(2,1)} %get-tuple-element.109.dy_ref), custom_call_target="tpu_custom_call" | custom-call | flops 8858370048 | bytes 25165824 | tf_op jit(solution)/shard_map/ffn_gradient/pallas_call | solution.py:555
  312.4 16.0 %collective-permute-done.38 = bf16[128,2048]{1,0:T(8,128)(2,1)} collective-permute-done((bf16[128,2048]{1,0:T(8,128)(2,1)}, bf16[128,2048]{1,0:T(8,128)(2,1)}, u32[]{:S(2)}, u32[]{:S(2)}) %collective-permute-start.38) | collective-permute-done | bytes 524320 | tf_op jit(solution)/shard_map/ppermute | solution.py:54
  335.4 9.5 %collective-permute-done.43 = bf16[128,2048]{1,0:T(8,128)(2,1)S(1)} collective-permute-done((bf16[128,2048]{1,0:T(8,128)(2,1)S(1)}, bf16[128,2048]{1,0:T(8,128)(2,1)S(1)}, u32[]{:S(2)}, u32[]{:S(2)}) %collective-permute-start.43) | collective-permute-done | bytes 524320 | tf_op jit(solution)/shard_map/ppermute | solution.py:54
  362.5 12.5 %attend_back.1 = (bf16[512,1024]{1,0:T(8,128)(2,1)}, bf16[4,2048,128]{2,1,0:T(8,128)(2,1)}) custom-call(s32[4]{0:T(128)} %pad_add_fusion.refs_0_, bf16[512,1024]{1,0:T(8,128)(2,1)} %get-tuple-element.125.refs_1_, bf16[2048,256]{1,0:T(8,128)(2,1)} %get-tuple-element.126.refs_2_, bf16[2048,256]{1,0:T(8,128)(2,1)} %get-tuple-element.127.refs_3_, ...), custom_call_target="tpu_custom_call" | custom-call | flops 10737418240 | bytes 12582912 | tf_op jit(solution)/shard_map/attend_back/pallas_call | solution.py:410
  387.5 7.1 %collective-permute-start.56 = (bf16[384,1024]{1,0:T(8,128)(2,1)S(1)}, bf16[384,1024]{1,0:T(8,128)(2,1)S(1)}, u32[]{:S(2)}, u32[]{:S(2)}) collective-permute-start(bf16[384,1024]{1,0:T(8,128)(2,1)S(1)} %constant_dynamic-slice_fusion.9), channel_id=1, source_target_pairs={{0,4},{4,8},{8,12},{12,0},{1,5},{5,9},{9,13},{13,1},{2,6},{6,10},{... | collective-permute-start | bytes 2359304 | tf_op jit(solution)/shard_map/ppermute | solution.py:54
  395.8 7.7 %collective-permute-done.46 = bf16[2048,128]{1,0:T(8,128)(2,1)S(1)} collective-permute-done((bf16[2048,128]{1,0:T(8,128)(2,1)S(1)}, bf16[2048,128]{1,0:T(8,128)(2,1)S(1)}, u32[]{:S(2)}, u32[]{:S(2)}) %collective-permute-start.46) | collective-permute-done | bytes 524320 | tf_op jit(solution)/shard_map/ppermute | solution.py:71
  405.2 15.5 %collective-permute-done.48 = bf16[2048,128]{1,0:T(8,128)(2,1)S(1)} collective-permute-done((bf16[2048,128]{1,0:T(8,128)(2,1)S(1)}, bf16[2048,128]{1,0:T(8,128)(2,1)S(1)}, u32[]{:S(2)}, u32[]{:S(2)}) %collective-permute-start.48) | collective-permute-done | bytes 524320 | tf_op jit(solution)/shard_map/ppermute | solution.py:70
  426.4 8.4 %collective-permute-done.49 = bf16[128,1024]{1,0:T(8,128)(2,1)S(1)} collective-permute-done((bf16[128,1024]{1,0:T(8,128)(2,1)S(1)}, bf16[128,1024]{1,0:T(8,128)(2,1)S(1)}, u32[]{:S(2)}, u32[]{:S(2)}) %collective-permute-start.49) | collective-permute-done | bytes 262176 | tf_op jit(solution)/shard_map/ppermute | solution.py:71
  437.6 6.4 %collective-permute-done.51 = bf16[128,1024]{1,0:T(8,128)(2,1)S(1)} collective-permute-done((bf16[128,1024]{1,0:T(8,128)(2,1)S(1)}, bf16[128,1024]{1,0:T(8,128)(2,1)S(1)}, u32[]{:S(2)}, u32[]{:S(2)}) %collective-permute-start.51) | collective-permute-done | bytes 262176 | tf_op jit(solution)/shard_map/ppermute | solution.py:70
  446.3 5.3 collective-permute-done.57
  455.4 4.6 collective-permute-done.58
  479.0 4.7 fusion.4
  512.0 8.3 %collective-permute-done.63 = bf16[320,384]{1,0:T(8,128)(2,1)S(1)} collective-permute-done((bf16[320,384]{1,0:T(8,128)(2,1)S(1)}, bf16[320,384]{1,0:T(8,128)(2,1)S(1)}, u32[]{:S(2)}, u32[]{:S(2)}) %collective-permute-start.63) | collective-permute-done | bytes 245792 | tf_op jit(solution)/shard_map/ppermute | solution.py:54
  524.3 4.7 collective-permute-done.67
  530.4 7.1 %collective-permute-done.68 = bf16[320,384]{1,0:T(8,128)(2,1)S(1)} collective-permute-done((bf16[320,384]{1,0:T(8,128)(2,1)S(1)}, bf16[320,384]{1,0:T(8,128)(2,1)S(1)}, u32[]{:S(2)}, u32[]{:S(2)}) %collective-permute-start.68) | collective-permute-done | bytes 245792 | tf_op jit(solution)/shard_map/ppermute | solution.py:54
  541.3 5.9 %collective-permute-done.65 = bf16[128,2048]{1,0:T(8,128)(2,1)S(1)} collective-permute-done((bf16[128,2048]{1,0:T(8,128)(2,1)S(1)}, bf16[128,2048]{1,0:T(8,128)(2,1)S(1)}, u32[]{:S(2)}, u32[]{:S(2)}) %collective-permute-start.65) | collective-permute-done | bytes 524320 | tf_op jit(solution)/shard_map/ppermute | solution.py:71
  (460 shorter events, 246.5 us)
Async XLA Ops:
  7.2 164.6 %all-gather.3.cloned.1.call-start = ((), (), s32[]{:S(2)}) async-start(), calls=%async_computation.1 | async-start | bytes 19464192 | tf_op jit(solution)/shard_map/all_gather | solution.py:624
  10.4 230.3 %all-gather.5.cloned.1.call-start = ((), (), s32[]{:S(2)}) async-start(), calls=%async_computation.2 | async-start | bytes 2621440 | tf_op jit(solution)/shard_map/all_gather | solution.py:640
  12.2 19.9 %collective-permute-start.3 = (bf16[96,1024]{1,0:T(8,128)(2,1)S(1)}, bf16[96,1024]{1,0:T(8,128)(2,1)S(1)}, u32[]{:S(2)}, u32[]{:S(2)}) collective-permute-start(bf16[96,1024]{1,0:T(8,128)(2,1)S(1)} %get-tuple-element.180), channel_id=1, source_target_pairs={{0,1},{1,0},{2,3},{3,2},{4,5},{5,4},{6,7},{7,6},{8,9},{9,8},{10,11... | collective-permute-start | bytes 589832 | tf_op jit(solution)/shard_map/ppermute | solution.py:71
  26.8 24.1 %collective-permute-start.10 = (bf16[320,384]{1,0:T(8,128)(2,1)}, bf16[320,384]{1,0:T(8,128)(2,1)S(1)}, u32[]{:S(2)}, u32[]{:S(2)}) collective-permute-start(bf16[320,384]{1,0:T(8,128)(2,1)} %bitcast.256), channel_id=1, source_target_pairs={{0,8},{4,12},{8,0},{12,4},{1,9},{5,13},{9,1},{13,5},{2,10},{6,14},... | collective-permute-start | bytes 737288 | tf_op jit(solution)/shard_map/ppermute | solution.py:54
  29.4 21.5 %collective-permute-start.11 = (bf16[320,384]{1,0:T(8,128)(2,1)}, bf16[320,384]{1,0:T(8,128)(2,1)S(1)}, u32[]{:S(2)}, u32[]{:S(2)}) collective-permute-start(bf16[320,384]{1,0:T(8,128)(2,1)} %bitcast.257), channel_id=1, source_target_pairs={{0,12},{4,0},{8,4},{12,8},{1,13},{5,1},{9,5},{13,9},{2,14},{6,2},{... | collective-permute-start | bytes 737288 | tf_op jit(solution)/shard_map/ppermute | solution.py:54
  30.8 20.2 %collective-permute-start.9 = (bf16[320,384]{1,0:T(8,128)(2,1)}, bf16[320,384]{1,0:T(8,128)(2,1)S(1)}, u32[]{:S(2)}, u32[]{:S(2)}) collective-permute-start(bf16[320,384]{1,0:T(8,128)(2,1)} %bitcast.258), channel_id=1, source_target_pairs={{0,4},{4,8},{8,12},{12,0},{1,5},{5,9},{9,13},{13,1},{2,6},{6,10},{... | collective-permute-start | bytes 737288 | tf_op jit(solution)/shard_map/ppermute | solution.py:54
  54.1 29.8 %collective-permute-start.1 = (bf16[128,2048]{1,0:T(8,128)(2,1)S(1)}, bf16[128,2048]{1,0:T(8,128)(2,1)S(1)}, u32[]{:S(2)}, u32[]{:S(2)}) collective-permute-start(bf16[128,2048]{1,0:T(8,128)(2,1)S(1)} %bitcast.225), channel_id=1, source_target_pairs={{0,2},{2,0},{1,3},{3,1},{4,6},{6,4},{5,7},{7,5},{8,10},{10,8},{9,1... | collective-permute-start | bytes 1572872 | tf_op jit(solution)/shard_map/ppermute | solution.py:71
  54.9 30.6 %collective-permute-start.2 = (bf16[128,2048]{1,0:T(8,128)(2,1)S(1)}, bf16[128,2048]{1,0:T(8,128)(2,1)}, u32[]{:S(2)}, u32[]{:S(2)}) collective-permute-start(bf16[128,2048]{1,0:T(8,128)(2,1)S(1)} %bitcast.226), channel_id=1, source_target_pairs={{0,3},{1,2},{2,1},{3,0},{4,7},{5,6},{6,5},{7,4},{8,11},{9,10},{10,... | collective-permute-start | bytes 1572872 | tf_op jit(solution)/shard_map/ppermute | solution.py:70
  59.7 34.1 %collective-permute-start.12 = (bf16[1280,384]{1,0:T(8,128)(2,1)}, bf16[1280,384]{1,0:T(8,128)(2,1)}, u32[]{:S(2)}, u32[]{:S(2)}) collective-permute-start(bf16[1280,384]{1,0:T(8,128)(2,1)} %bitcast.235), channel_id=1, source_target_pairs={{0,16},{16,0},{1,17},{17,1},{2,18},{18,2},{3,19},{19,3},{4,20},{20... | collective-permute-start | bytes 2949128 | tf_op jit(solution)/shard_map/ppermute | solution.py:54
  70.4 21.0 %collective-permute-start.21 = (bf16[128,1024]{1,0:T(8,128)(2,1)}, bf16[128,1024]{1,0:T(8,128)(2,1)S(1)}, u32[]{:S(2)}, u32[]{:S(2)}) collective-permute-start(bf16[128,1024]{1,0:T(8,128)(2,1)} %collective-permute-done.20), channel_id=1, source_target_pairs={{0,4},{4,8},{8,12},{12,0},{1,5},{5,9},{9,13},{13,1},{2,6},{6,10},{... | collective-permute-start | bytes 786440 | tf_op jit(solution)/shard_map/ppermute | solution.py:54
  119.5 20.2 %collective-permute-start.14 = (bf16[512,128]{1,0:T(8,128)(2,1)S(1)}, bf16[512,128]{1,0:T(8,128)(2,1)S(1)}, u32[]{:S(2)}, u32[]{:S(2)}) collective-permute-start(bf16[512,128]{1,0:T(8,128)(2,1)S(1)} %get-tuple-element.186), channel_id=1, source_target_pairs={{0,8},{4,12},{8,0},{12,4},{1,9},{5,13},{9,1},{13,5},{2,10},{6,14},... | collective-permute-start | bytes 393224 | tf_op jit(solution)/shard_map/ppermute | solution.py:54
  122.8 20.1 %collective-permute-start.15 = (bf16[512,128]{1,0:T(8,128)(2,1)S(1)}, bf16[512,128]{1,0:T(8,128)(2,1)}, u32[]{:S(2)}, u32[]{:S(2)}) collective-permute-start(bf16[512,128]{1,0:T(8,128)(2,1)S(1)} %get-tuple-element.186), channel_id=1, source_target_pairs={{0,12},{4,0},{8,4},{12,8},{1,13},{5,1},{9,5},{13,9},{2,14},{6,2},{... | collective-permute-start | bytes 393224 | tf_op jit(solution)/shard_map/ppermute | solution.py:54
  134.3 32.5 %collective-permute-start.26 = (bf16[1024,1024]{1,0:T(8,128)(2,1)}, bf16[1024,1024]{1,0:T(8,128)(2,1)}, u32[]{:S(2)}, u32[]{:S(2)}) collective-permute-start(bf16[1024,1024]{1,0:T(8,128)(2,1)} %bitcast.227), channel_id=1, source_target_pairs={{0,16},{16,0},{1,17},{17,1},{2,18},{18,2},{3,19},{19,3},{4,20},{20... | collective-permute-start | bytes 6291464 | tf_op jit(solution)/shard_map/ppermute | solution.py:54
  137.2 21.8 %collective-permute-start.22 = (bf16[512,1024]{1,0:T(8,128)(2,1)}, bf16[512,1024]{1,0:T(8,128)(2,1)}, u32[]{:S(2)}, u32[]{:S(2)}) collective-permute-start(bf16[512,1024]{1,0:T(8,128)(2,1)} %bitcast.231), channel_id=1, source_target_pairs={{0,16},{16,0},{1,17},{17,1},{2,18},{18,2},{3,19},{19,3},{4,20},{20... | collective-permute-start | bytes 3145736 | tf_op jit(solution)/shard_map/ppermute | solution.py:54
  156.1 24.3 %collective-permute-start.28 = (bf16[2048,128]{1,0:T(8,128)(2,1)}, bf16[2048,128]{1,0:T(8,128)(2,1)}, u32[]{:S(2)}, u32[]{:S(2)}) collective-permute-start(bf16[2048,128]{1,0:T(8,128)(2,1)} %bitcast.273), channel_id=1, source_target_pairs={{0,2},{2,0},{1,3},{3,1},{4,6},{6,4},{5,7},{7,5},{8,10},{10,8},{9,1... | collective-permute-start | bytes 1572872 | tf_op jit(solution)/shard_map/ppermute | solution.py:71
  156.8 23.6 %collective-permute-start.29 = (bf16[2048,128]{1,0:T(8,128)(2,1)}, bf16[2048,128]{1,0:T(8,128)(2,1)}, u32[]{:S(2)}, u32[]{:S(2)}) collective-permute-start(bf16[2048,128]{1,0:T(8,128)(2,1)} %bitcast.274), channel_id=1, source_target_pairs={{0,3},{1,2},{2,1},{3,0},{4,7},{5,6},{6,5},{7,4},{8,11},{9,10},{10,... | collective-permute-start | bytes 1572872 | tf_op jit(solution)/shard_map/ppermute | solution.py:70
  171.8 380.7 %reduce-scatter.2.cloned.1.call-start = ((), (), s32[]{:S(2)}) async-start(), calls=%async_computation.3 | async-start | bytes 19464192 | tf_op jit(solution)/shard_map/reduce_scatter | solution.py:699
  198.6 23.2 %collective-permute-start.31 = (bf16[128,2048]{1,0:T(8,128)(2,1)}, bf16[128,2048]{1,0:T(8,128)(2,1)S(1)}, u32[]{:S(2)}, u32[]{:S(2)}) collective-permute-start(bf16[128,2048]{1,0:T(8,128)(2,1)} %get-tuple-element.159), channel_id=1, source_target_pairs={{0,2},{2,0},{1,3},{3,1},{4,6},{6,4},{5,7},{7,5},{8,10},{10,8},{9,1... | collective-permute-start | bytes 1572872 | tf_op jit(solution)/shard_map/ppermute | solution.py:71
  200.0 22.7 %collective-permute-start.32 = (bf16[128,2048]{1,0:T(8,128)(2,1)}, bf16[128,2048]{1,0:T(8,128)(2,1)}, u32[]{:S(2)}, u32[]{:S(2)}) collective-permute-start(bf16[128,2048]{1,0:T(8,128)(2,1)} %get-tuple-element.158), channel_id=1, source_target_pairs={{0,3},{1,2},{2,1},{3,0},{4,7},{5,6},{6,5},{7,4},{8,11},{9,10},{10,... | collective-permute-start | bytes 1572872 | tf_op jit(solution)/shard_map/ppermute | solution.py:70
  238.1 20.6 %collective-permute-start.34 = (bf16[128,2048]{1,0:T(8,128)(2,1)}, bf16[128,2048]{1,0:T(8,128)(2,1)}, u32[]{:S(2)}, u32[]{:S(2)}) collective-permute-start(bf16[128,2048]{1,0:T(8,128)(2,1)} %collective-permute-done.33.refs_2_), channel_id=1, source_target_pairs={{0,4},{4,8},{8,12},{12,0},{1,5},{5,9},{9,13},{13,1},{2,6},{6,10},{... | collective-permute-start | bytes 1572872 | tf_op jit(solution)/shard_map/ppermute | solution.py:54
  261.0 32.5 %collective-permute-start.36 = (bf16[128,2048]{1,0:T(8,128)(2,1)}, bf16[128,2048]{1,0:T(8,128)(2,1)S(1)}, u32[]{:S(2)}, u32[]{:S(2)}) collective-permute-start(bf16[128,2048]{1,0:T(8,128)(2,1)} %get-tuple-element.110), channel_id=1, source_target_pairs={{0,4},{4,8},{8,12},{12,0},{1,5},{5,9},{9,13},{13,1},{2,6},{6,10},{... | collective-permute-start | bytes 1572872 | tf_op jit(solution)/shard_map/ppermute | solution.py:54
  356.9 26.0 %collective-permute-start.42 = (bf16[1024,1024]{1,0:T(8,128)(2,1)}, bf16[1024,1024]{1,0:T(8,128)(2,1)}, u32[]{:S(2)}, u32[]{:S(2)}) collective-permute-start(bf16[1024,1024]{1,0:T(8,128)(2,1)} %convolution_convert_fusion), channel_id=1, source_target_pairs={{0,16},{16,0},{1,17},{17,1},{2,18},{18,2},{3,19},{19,3},{4,20},{20... | collective-permute-start | bytes 6291464 | tf_op jit(solution)/shard_map/ppermute | solution.py:54
  377.5 26.1 %collective-permute-start.46 = (bf16[2048,128]{1,0:T(8,128)(2,1)S(1)}, bf16[2048,128]{1,0:T(8,128)(2,1)S(1)}, u32[]{:S(2)}, u32[]{:S(2)}) collective-permute-start(bf16[2048,128]{1,0:T(8,128)(2,1)S(1)} %get-tuple-element.165), channel_id=1, source_target_pairs={{0,1},{1,0},{2,3},{3,2},{4,5},{5,4},{6,7},{7,6},{8,9},{9,8},{10,11... | collective-permute-start | bytes 1572872 | tf_op jit(solution)/shard_map/ppermute | solution.py:71
  378.8 26.4 %collective-permute-start.47 = (bf16[2048,128]{1,0:T(8,128)(2,1)S(1)}, bf16[2048,128]{1,0:T(8,128)(2,1)S(1)}, u32[]{:S(2)}, u32[]{:S(2)}) collective-permute-start(bf16[2048,128]{1,0:T(8,128)(2,1)S(1)} %get-tuple-element.167), channel_id=1, source_target_pairs={{0,2},{2,0},{1,3},{3,1},{4,6},{6,4},{5,7},{7,5},{8,10},{10,8},{9,1... | collective-permute-start | bytes 1572872 | tf_op jit(solution)/shard_map/ppermute | solution.py:71
  378.8 41.8 %collective-permute-start.48 = (bf16[2048,128]{1,0:T(8,128)(2,1)S(1)}, bf16[2048,128]{1,0:T(8,128)(2,1)S(1)}, u32[]{:S(2)}, u32[]{:S(2)}) collective-permute-start(bf16[2048,128]{1,0:T(8,128)(2,1)S(1)} %get-tuple-element.166), channel_id=1, source_target_pairs={{0,3},{1,2},{2,1},{3,0},{4,7},{5,6},{6,5},{7,4},{8,11},{9,10},{10,... | collective-permute-start | bytes 1572872 | tf_op jit(solution)/shard_map/ppermute | solution.py:70
  387.5 37.1 %collective-permute-start.56 = (bf16[384,1024]{1,0:T(8,128)(2,1)S(1)}, bf16[384,1024]{1,0:T(8,128)(2,1)S(1)}, u32[]{:S(2)}, u32[]{:S(2)}) collective-permute-start(bf16[384,1024]{1,0:T(8,128)(2,1)S(1)} %constant_dynamic-slice_fusion.9), channel_id=1, source_target_pairs={{0,4},{4,8},{8,12},{12,0},{1,5},{5,9},{9,13},{13,1},{2,6},{6,10},{... | collective-permute-start | bytes 2359304 | tf_op jit(solution)/shard_map/ppermute | solution.py:54
  422.0 21.9 %collective-permute-start.51 = (bf16[128,1024]{1,0:T(8,128)(2,1)S(1)}, bf16[128,1024]{1,0:T(8,128)(2,1)S(1)}, u32[]{:S(2)}, u32[]{:S(2)}) collective-permute-start(bf16[128,1024]{1,0:T(8,128)(2,1)S(1)} %get-tuple-element.163), channel_id=1, source_target_pairs={{0,3},{1,2},{2,1},{3,0},{4,7},{5,6},{6,5},{7,4},{8,11},{9,10},{10,... | collective-permute-start | bytes 786440 | tf_op jit(solution)/shard_map/ppermute | solution.py:70
  424.9 27.3 %collective-permute-start.60 = (bf16[384,1024]{1,0:T(8,128)(2,1)S(1)}, bf16[384,1024]{1,0:T(8,128)(2,1)S(1)}, u32[]{:S(2)}, u32[]{:S(2)}) collective-permute-start(bf16[384,1024]{1,0:T(8,128)(2,1)S(1)} %add_convert_fusion.4), channel_id=1, source_target_pairs={{0,4},{4,8},{8,12},{12,0},{1,5},{5,9},{9,13},{13,1},{2,6},{6,10},{... | collective-permute-start | bytes 2359304 | tf_op jit(solution)/shard_map/ppermute | solution.py:54
  453.3 23.1 %collective-permute-start.61 = (bf16[384,1024]{1,0:T(8,128)(2,1)}, bf16[384,1024]{1,0:T(8,128)(2,1)}, u32[]{:S(2)}, u32[]{:S(2)}) collective-permute-start(bf16[384,1024]{1,0:T(8,128)(2,1)} %add_convert_fusion.3), channel_id=1, source_target_pairs={{0,4},{4,8},{8,12},{12,0},{1,5},{5,9},{9,13},{13,1},{2,6},{6,10},{... | collective-permute-start | bytes 2359304 | tf_op jit(solution)/shard_map/ppermute | solution.py:54
  489.3 19.7 %collective-permute-start.62 = (bf16[1280,384]{1,0:T(8,128)(2,1)}, bf16[1280,384]{1,0:T(8,128)(2,1)}, u32[]{:S(2)}, u32[]{:S(2)}) collective-permute-start(bf16[1280,384]{1,0:T(8,128)(2,1)} %bitcast.95), channel_id=1, source_target_pairs={{0,16},{16,0},{1,17},{17,1},{2,18},{18,2},{3,19},{19,3},{4,20},{20... | collective-permute-start | bytes 2949128 | tf_op jit(solution)/shard_map/ppermute | solution.py:54
  521.8 25.4 %collective-permute-start.65 = (bf16[128,2048]{1,0:T(8,128)(2,1)S(1)}, bf16[128,2048]{1,0:T(8,128)(2,1)S(1)}, u32[]{:S(2)}, u32[]{:S(2)}) collective-permute-start(bf16[128,2048]{1,0:T(8,128)(2,1)S(1)} %get-tuple-element.156), channel_id=1, source_target_pairs={{0,2},{2,0},{1,3},{3,1},{4,6},{6,4},{5,7},{7,5},{8,10},{10,8},{9,1... | collective-permute-start | bytes 1572872 | tf_op jit(solution)/shard_map/ppermute | solution.py:71
  522.8 24.4 %collective-permute-start.66 = (bf16[128,2048]{1,0:T(8,128)(2,1)S(1)}, bf16[128,2048]{1,0:T(8,128)(2,1)S(1)}, u32[]{:S(2)}, u32[]{:S(2)}) collective-permute-start(bf16[128,2048]{1,0:T(8,128)(2,1)S(1)} %get-tuple-element.155), channel_id=1, source_target_pairs={{0,3},{1,2},{2,1},{3,0},{4,7},{5,6},{6,5},{7,4},{8,11},{9,10},{10,... | collective-permute-start | bytes 1572872 | tf_op jit(solution)/shard_map/ppermute | solution.py:70
  (135 other events, 1414.2 us)
Sparse Core Ops, SparseCore 0:
  10.5 118.0 all-gather.2
  171.9 43.5 all-gather.4
  311.9 148.0 reduce-scatter.1
where the time goes:
time: 576 us; the launch traced here: 565 us
  waiting for transfers between devices  233 us (40%)
  Pallas kernels  117 us (20%)
  starting transfers between devices  90.4 us (16%)
  other arithmetic  48.7 us (8%)
  matrix products  31.2 us (5%)
  local copies, waits for them, and re-layouts  29.4 us (5%)
  between operations  15.5 us (3%)
    ppermute x36, waiting for transfers between devices, shift(): lax.ppermute(value, axis, [(i, (i + by) % count) for i in range(count)])  111 us
    ppermute x26, waiting for transfers between devices, flip(): return lax.ppermute(value, 'px' if by == 1 else 'py', [(0, 1), (1, 0)])  93.3 us
    pallas_call x13, Pallas kernels, place(): pl.pallas_call(kernel, grid_spec=pltpu.PrefetchScalarGridSpec(num_scalar_...  41.4 us
    ppermute x36, starting transfers between devices, shift(): lax.ppermute(value, axis, [(i, (i + by) % count) for i in range(count)])  39.9 us
    pallas_call x2, Pallas kernels, feed_forward(): pl.pallas_call(lambda *refs: ffn_kernel(chunk, count, blocks, *refs), gri...  36 us
    ppermute x26, starting transfers between devices, flip(): return lax.ppermute(value, 'px' if by == 1 else 'py', [(0, 1), (1, 0)])  32.1 us
    ppermute x13, waiting for transfers between devices, flip(): return lax.ppermute(value, ('py', 'px'), [(i, i ^ 3) for i in range(PLANE)])  28.7 us
    ppermute x13, starting transfers between devices, flip(): return lax.ppermute(value, ('py', 'px'), [(i, i ^ 3) for i in range(PLANE)])  18 us
  transfers between devices with their start and end apart: 78, of which 35 were waited for; matrix products, arithmetic and copies ran while one was open for 15% of the time, Pallas kernels for 21%

commit v1 on v0

--- a/solution.py
+++ b/solution.py
@@ -620,9 +620,10 @@
     hidden_axes = ("rows", "py", "px")
     down_w = column_swap(jnp.concatenate([down_w, gains]), plane)
     ffn_w = jnp.concatenate([jnp.transpose(w_gate), jnp.transpose(w_up), w_down])
-    token_blocks = plane_spread(own_tokens)
+    group_tokens = lax.all_gather(own_tokens, ("py", "px"), axis=0, tiled=True)
+    down_ring = ring_spread(down_w, "ring")
+    ffn_w, group_tokens, *down_ring = tie(ffn_w, group_tokens, *down_ring)
     ffn_w = lax.all_gather(ffn_w, hidden_axes, axis=0, tiled=True)
-    down_ring = ring_spread(down_w, "ring")
     other_w = jnp.concatenate([w_qup, jnp.transpose(w_out)])
     other_w = column_swap(other_w, plane)
     other_w = other_w.reshape(PLANE, -1, other_w.shape[1])
@@ -649,7 +650,7 @@
     key_cos, key_sin = rope_tables(key_relative, HD // 2)
     scal = jnp.concatenate([jnp.stack([plane, ring * group]), doc_lengths[0]]).astype(jnp.int32)
 
-    group_tokens = plane_place(token_blocks, plane).astype(F32)
+    group_tokens = group_tokens.astype(F32)
     normed = rms_norm(group_tokens, gain_attn).astype(BF)
     projected = mm(normed, down_w).astype(BF)
 
@@ -761,11 +762,14 @@
     gain_grads = jnp.pad(gain_grads[:, None], ((0, 0), (0, EXTRA - 1), (0, lanes - gain_count)))
     gain_grads = gain_grads.reshape(rows, rings * PLANE, EXTRA, lanes)
     grad_down = over_rows(row_blocks(normed, grad_projected, spot, gain_grads))
+    grad_down, wide_grad = tie(grad_down, wide_grad)
     down_parts = ring_parts(grad_down, spot)
     ffn_grad = ffn_grad.astype(F32).reshape(3, -1, ffn_grad.shape[1])
     gate_grad, up_grad, down_grad = jnp.transpose(ffn_grad[0]), jnp.transpose(ffn_grad[1]), ffn_grad[2]
     grad_down = ring_steps(down_parts, 1, 1)
-    grad_down, grad_normed = tie(grad_down, grad_normed)
+    grad_down, grad_normed, gate_grad, up_grad, down_grad = tie(
+        grad_down, grad_normed, gate_grad, up_grad, down_grad
+    )
     grad_down = ring_steps(down_parts, 2, rings - 1, grad_down)
     grad_down = grad_down.astype(BF)
     grad_up_query, grad_out_w = over_plane(wide_grad, spot, up_rows)

time: 576 us -> 573 us (level)
  starting transfers between devices: 90.4 us -> 77.6 us
  local copies, waits for them, and re-layouts: 29.4 us -> 38.9 us
  waiting for transfers between devices: 233 us -> 240 us
    ppermute x36, waiting for transfers between devices: 111 us -> 135 us  [shift(): lax.ppermute(value, axis, [(i, (i + by) % count) for i in range(count)])]
    ppermute x26 -> x24, waiting for transfers between devices: 93.3 us -> 71.4 us  [flip(): return lax.ppermute(value, 'px' if by == 1 else 'py', [(0, 1), (1, 0)])]
    unnamed x188 -> x186, local copies, waits for them, and re-layouts: 12.9 us -> 20 us
    ppermute x36, starting transfers between devices: 39.9 us -> 32.9 us  [shift(): lax.ppermute(value, axis, [(i, (i + by) % count) for i in range(count)])]
    pallas_call x13 -> x12, Pallas kernels: 41.4 us -> 37.9 us  [place(): pl.pallas_call(kernel, grid_spec=pltpu.PrefetchScalarGridSpec(num_scalar_...]
    ppermute x26 -> x24, starting transfers between devices: 32.1 us -> 28.9 us  [flip(): return lax.ppermute(value, 'px' if by == 1 else 'py', [(0, 1), (1, 0)])]
    ppermute x13 -> x12, starting transfers between devices: 18 us -> 15.4 us  [flip(): return lax.ppermute(value, ('py', 'px'), [(i, i ^ 3) for i in range(PLANE)])]
    ppermute x13 -> x12, waiting for transfers between devices: 28.7 us -> 30 us  [flip(): return lax.ppermute(value, ('py', 'px'), [(i, i ^ 3) for i in range(PLANE)])]
  transfers between devices with their start and end apart: 78 -> 76, of which waited for: 35 -> 41; matrix products, arithmetic and copies ran while one was open for 15% -> 17% of each run, Pallas kernels for 21% -> 20%
where the time goes in v1:
time: 573 us; the launch traced here: 564 us
  waiting for transfers between devices  240 us (42%)
  Pallas kernels  113 us (20%)
  starting transfers between devices  77.6 us (14%)
  other arithmetic  48.8 us (9%)
  local copies, waits for them, and re-layouts  38.9 us (7%)
  matrix products  30.6 us (5%)
  between operations  15.7 us (3%)
    ppermute x36, waiting for transfers between devices, shift(): lax.ppermute(value, axis, [(i, (i + by) % count) for i in range(count)])  135 us
    ppermute x24, waiting for transfers between devices, flip(): return lax.ppermute(value, 'px' if by == 1 else 'py', [(0, 1), (1, 0)])  71.4 us
    pallas_call x12, Pallas kernels, place(): pl.pallas_call(kernel, grid_spec=pltpu.PrefetchScalarGridSpec(num_scalar_...  37.9 us
    pallas_call x2, Pallas kernels, feed_forward(): pl.pallas_call(lambda *refs: ffn_kernel(chunk, count, blocks, *refs), gri...  36 us
    ppermute x36, starting transfers between devices, shift(): lax.ppermute(value, axis, [(i, (i + by) % count) for i in range(count)])  32.9 us
    ppermute x12, waiting for transfers between devices, flip(): return lax.ppermute(value, ('py', 'px'), [(i, i ^ 3) for i in range(PLANE)])  30 us
    ppermute x24, starting transfers between devices, flip(): return lax.ppermute(value, 'px' if by == 1 else 'py', [(0, 1), (1, 0)])  28.9 us
    unnamed x186, local copies, waits for them, and re-layouts  20 us
  transfers between devices with their start and end apart: 76, of which 41 were waited for; matrix products, arithmetic and copies ran while one was open for 17% of the time, Pallas kernels for 20%

profile of v1, /device:TPU:0, one launch (start us, length us, event | category | flops | bytes accessed | tf_op | source)
XLA Modules:
  0.0 564.5 jit_solution(11625077261062853116)
XLA Ops:
  39.9 6.9 %collective-permute-done.4 = bf16[320,384]{1,0:T(8,128)(2,1)S(1)} collective-permute-done((bf16[320,384]{1,0:T(8,128)(2,1)}, bf16[320,384]{1,0:T(8,128)(2,1)S(1)}, u32[]{:S(2)}, u32[]{:S(2)}) %collective-permute-start.4) | collective-permute-done | bytes 245792 | tf_op jit(solution)/shard_map/ppermute | solution.py:54
  66.7 5.1 collective-permute-start.16
  78.5 7.5 %collective-permute-done.17 = bf16[128,1024]{1,0:T(8,128)(2,1)S(1)} collective-permute-done((bf16[128,1024]{1,0:T(8,128)(2,1)S(1)}, bf16[128,1024]{1,0:T(8,128)(2,1)S(1)}, u32[]{:S(2)}, u32[]{:S(2)}) %collective-permute-start.17) | collective-permute-done | bytes 262176 | tf_op jit(solution)/shard_map/ppermute | solution.py:54
  88.1 7.2 %collective-permute-done.18 = bf16[128,1024]{1,0:T(8,128)(2,1)S(1)} collective-permute-done((bf16[128,1024]{1,0:T(8,128)(2,1)S(1)}, bf16[128,1024]{1,0:T(8,128)(2,1)S(1)}, u32[]{:S(2)}, u32[]{:S(2)}) %collective-permute-start.18) | collective-permute-done | bytes 262176 | tf_op jit(solution)/shard_map/ppermute | solution.py:54
  100.6 9.6 %collective-permute-done.20 = bf16[256,1024]{1,0:T(8,128)(2,1)S(1)} collective-permute-done((bf16[256,1024]{1,0:T(8,128)(2,1)S(1)}, bf16[256,1024]{1,0:T(8,128)(2,1)S(1)}, u32[]{:S(2)}, u32[]{:S(2)}) %collective-permute-start.20) | collective-permute-done | bytes 524320 | tf_op jit(solution)/shard_map/ppermute | solution.py:54
  111.0 12.4 %collective-permute-done.21 = bf16[256,1024]{1,0:T(8,128)(2,1)S(1)} collective-permute-done((bf16[256,1024]{1,0:T(8,128)(2,1)S(1)}, bf16[256,1024]{1,0:T(8,128)(2,1)S(1)}, u32[]{:S(2)}, u32[]{:S(2)}) %collective-permute-start.21) | collective-permute-done | bytes 524320 | tf_op jit(solution)/shard_map/ppermute | solution.py:54
  125.3 4.4 collective-permute-start.11
  129.7 10.3 %collective-permute-done.22 = bf16[256,1024]{1,0:T(8,128)(2,1)S(1)} collective-permute-done((bf16[256,1024]{1,0:T(8,128)(2,1)S(1)}, bf16[256,1024]{1,0:T(8,128)(2,1)S(1)}, u32[]{:S(2)}, u32[]{:S(2)}) %collective-permute-start.22) | collective-permute-done | bytes 524320 | tf_op jit(solution)/shard_map/ppermute | solution.py:54
  151.6 5.5 multiply_sine_fusion
  176.7 5.0 place.20
  182.0 5.8 %collective-permute-done.25.refs_4_ = bf16[2048,128]{1,0:T(8,128)(2,1)} collective-permute-done((bf16[2048,128]{1,0:T(8,128)(2,1)}, bf16[2048,128]{1,0:T(8,128)(2,1)}, u32[]{:S(2)}, u32[]{:S(2)}) %collective-permute-start.25) | collective-permute-done | bytes 524320 | tf_op jit(solution)/shard_map/ppermute | solution.py:71
  187.8 10.8 %attend.1 = (bf16[512,1024]{1,0:T(8,128)(2,1)}, bf16[512,1024]{1,0:T(8,128)(2,1)}, f32[512,512]{1,0:T(8,128)}, bf16[2048,256]{1,0:T(8,128)(2,1)}, bf16[2048,256]{1,0:T(8,128)(2,1)}) custom-call(s32[4]{0:T(128)} %pad_add_fusion.refs_0_, f32[512,1024]{1,0:T(8,128)} %fusion.62.refs_1_, bf16[2048,128]{1,0:T(8,128)(2,1)} %bitcast.258, ...), custom_call_target="tpu_custom_call" | custom-call | flops 4294967296 | bytes 8388608 | tf_op jit(solution)/shard_map/attend/pallas_call | solution.py:317
  208.9 11.5 %collective-permute-done.27 = bf16[128,2048]{1,0:T(8,128)(2,1)S(1)} collective-permute-done((bf16[128,2048]{1,0:T(8,128)(2,1)}, bf16[128,2048]{1,0:T(8,128)(2,1)S(1)}, u32[]{:S(2)}, u32[]{:S(2)}) %collective-permute-start.27) | collective-permute-done | bytes 524320 | tf_op jit(solution)/shard_map/ppermute | solution.py:71
  220.4 8.9 %collective-permute-done.28 = bf16[128,2048]{1,0:T(8,128)(2,1)S(1)} collective-permute-done((bf16[128,2048]{1,0:T(8,128)(2,1)}, bf16[128,2048]{1,0:T(8,128)(2,1)S(1)}, u32[]{:S(2)}, u32[]{:S(2)}) %collective-permute-start.28) | collective-permute-done | bytes 524320 | tf_op jit(solution)/shard_map/ppermute | solution.py:71
  234.8 10.9 %collective-permute-done.30.refs_2_ = bf16[128,2048]{1,0:T(8,128)(2,1)} collective-permute-done((bf16[128,2048]{1,0:T(8,128)(2,1)S(1)}, bf16[128,2048]{1,0:T(8,128)(2,1)}, u32[]{:S(2)}, u32[]{:S(2)}) %collective-permute-start.30) | collective-permute-done | bytes 524320 | tf_op jit(solution)/shard_map/ppermute | solution.py:54
  246.1 18.0 %feed_forward.2 = (bf16[3,512,1408]{2,1,0:T(8,128)(2,1)}, bf16[512,2048]{1,0:T(8,128)(2,1)}, bf16[512,2048]{1,0:T(8,128)(2,1)}, bf16[128,2048]{1,0:T(8,128)(2,1)...) custom-call(s32[2]{0:T(128)} %and_select_fusion.refs_0_, ...), custom_call_target="tpu_custom_call" | custom-call | flops 8858370048 | bytes 25165824 | tf_op jit(solution)/shard_map/feed_forward/pallas_call | solution.py:505
  265.4 15.7 %collective-permute-done.32.refs_2_ = bf16[128,2048]{1,0:T(8,128)(2,1)S(1)} collective-permute-done((bf16[128,2048]{1,0:T(8,128)(2,1)}, bf16[128,2048]{1,0:T(8,128)(2,1)S(1)}, u32[]{:S(2)}, u32[]{:S(2)}) %collective-permute-start.32) | collective-permute-done | bytes 524320 | tf_op jit(solution)/shard_map/ppermute | solution.py:54
  281.8 18.0 %feed_forward.3 = (bf16[3,512,1408]{2,1,0:T(8,128)(2,1)}, bf16[512,2048]{1,0:T(8,128)(2,1)}, bf16[512,2048]{1,0:T(8,128)(2,1)}, bf16[128,2048]{1,0:T(8,128)(2,1)...) custom-call(s32[2]{0:T(128)} %and_select_fusion.1.refs_0_, ...), custom_call_target="tpu_custom_call", output_to_operand_aliasing={{0}: (5, {}), {1}: (6, {}), {2}: (7, {})} | custom-call | flops 8858370048 | bytes 25165824 | tf_op jit(solution)/shard_map/feed_forward/pallas_call | solution.py:505
  301.1 16.1 %ffn_gradient.1 = bf16[2,4,3,352,1024]{4,3,2,1,0:T(8,128)(2,1)} custom-call(bf16[3,512,1408]{2,1,0:T(8,128)(2,1)} %get-tuple-element.124.left, bf16[512,2048]{1,0:T(8,128)(2,1)} %get-tuple-element.125.h_ref, bf16[512,2048]{1,0:T(8,128)(2,1)} %get-tuple-element.126.dy_ref), custom_call_target="tpu_custom_call" | custom-call | flops 8858370048 | bytes 25165824 | tf_op jit(solution)/shard_map/ffn_gradient/pallas_call | solution.py:555
  318.9 15.9 %collective-permute-done.35 = bf16[128,2048]{1,0:T(8,128)(2,1)} collective-permute-done((bf16[128,2048]{1,0:T(8,128)(2,1)}, bf16[128,2048]{1,0:T(8,128)(2,1)}, u32[]{:S(2)}, u32[]{:S(2)}) %collective-permute-start.35) | collective-permute-done | bytes 524320 | tf_op jit(solution)/shard_map/ppermute | solution.py:54
  341.9 9.9 %collective-permute-done.40 = bf16[128,2048]{1,0:T(8,128)(2,1)S(1)} collective-permute-done((bf16[128,2048]{1,0:T(8,128)(2,1)S(1)}, bf16[128,2048]{1,0:T(8,128)(2,1)S(1)}, u32[]{:S(2)}, u32[]{:S(2)}) %collective-permute-start.40) | collective-permute-done | bytes 524320 | tf_op jit(solution)/shard_map/ppermute | solution.py:54
  359.5 4.3 convolution_convert_fusion
  369.2 12.4 %attend_back.1 = (bf16[512,1024]{1,0:T(8,128)(2,1)}, bf16[4,2048,128]{2,1,0:T(8,128)(2,1)}) custom-call(s32[4]{0:T(128)} %pad_add_fusion.refs_0_, bf16[512,1024]{1,0:T(8,128)(2,1)} %get-tuple-element.142.refs_1_, bf16[2048,256]{1,0:T(8,128)(2,1)} %get-tuple-element.143.refs_2_, bf16[2048,256]{1,0:T(8,128)(2,1)} %get-tuple-element.144.refs_3_, ...), custom_call_target="tpu_custom_call" | custom-call | flops 10737418240 | bytes 12582912 | tf_op jit(solution)/shard_map/attend_back/pallas_call | solution.py:410
  394.3 6.0 %collective-permute-start.53 = (bf16[384,1024]{1,0:T(8,128)(2,1)S(1)}, bf16[384,1024]{1,0:T(8,128)(2,1)S(1)}, u32[]{:S(2)}, u32[]{:S(2)}) collective-permute-start(bf16[384,1024]{1,0:T(8,128)(2,1)S(1)} %constant_dynamic-slice_fusion.9), channel_id=1, source_target_pairs={{0,4},{4,8},{8,12},{12,0},{1,5},{5,9},{9,13},{13,1},{2,6},{6,10},{... | collective-permute-start | bytes 2359304 | tf_op jit(solution)/shard_map/ppermute | solution.py:54
  401.6 8.8 %collective-permute-done.43 = bf16[2048,128]{1,0:T(8,128)(2,1)S(1)} collective-permute-done((bf16[2048,128]{1,0:T(8,128)(2,1)S(1)}, bf16[2048,128]{1,0:T(8,128)(2,1)S(1)}, u32[]{:S(2)}, u32[]{:S(2)}) %collective-permute-start.43) | collective-permute-done | bytes 524320 | tf_op jit(solution)/shard_map/ppermute | solution.py:71
  411.3 15.8 %collective-permute-done.45 = bf16[2048,128]{1,0:T(8,128)(2,1)S(1)} collective-permute-done((bf16[2048,128]{1,0:T(8,128)(2,1)S(1)}, bf16[2048,128]{1,0:T(8,128)(2,1)S(1)}, u32[]{:S(2)}, u32[]{:S(2)}) %collective-permute-start.45) | collective-permute-done | bytes 524320 | tf_op jit(solution)/shard_map/ppermute | solution.py:70
  432.9 8.3 %collective-permute-done.46 = bf16[128,1024]{1,0:T(8,128)(2,1)S(1)} collective-permute-done((bf16[128,1024]{1,0:T(8,128)(2,1)S(1)}, bf16[128,1024]{1,0:T(8,128)(2,1)S(1)}, u32[]{:S(2)}, u32[]{:S(2)}) %collective-permute-start.46) | collective-permute-done | bytes 262176 | tf_op jit(solution)/shard_map/ppermute | solution.py:71
  443.9 6.5 %collective-permute-done.48 = bf16[128,1024]{1,0:T(8,128)(2,1)S(1)} collective-permute-done((bf16[128,1024]{1,0:T(8,128)(2,1)S(1)}, bf16[128,1024]{1,0:T(8,128)(2,1)S(1)}, u32[]{:S(2)}, u32[]{:S(2)}) %collective-permute-start.48) | collective-permute-done | bytes 262176 | tf_op jit(solution)/shard_map/ppermute | solution.py:70
  452.7 5.4 collective-permute-done.54
  461.8 4.6 collective-permute-done.55
  529.9 4.5 collective-permute-done.64
  535.4 7.2 %collective-permute-done.65 = bf16[320,384]{1,0:T(8,128)(2,1)S(1)} collective-permute-done((bf16[320,384]{1,0:T(8,128)(2,1)S(1)}, bf16[320,384]{1,0:T(8,128)(2,1)S(1)}, u32[]{:S(2)}, u32[]{:S(2)}) %collective-permute-start.65) | collective-permute-done | bytes 245792 | tf_op jit(solution)/shard_map/ppermute | solution.py:54
  (454 shorter events, 249.7 us)
Async XLA Ops:
  7.2 41.7 %all-gather.9.cloned.1.call-start = ((), (), s32[]{:S(2)}) async-start(), calls=%async_computation.4 | async-start | bytes 2621440 | tf_op jit(solution)/shard_map/all_gather | solution.py:623
  7.9 173.7 %all-gather.5.cloned.1.call-start = ((), (), s32[]{:S(2)}) async-start(), calls=%async_computation.1 | async-start | bytes 19464192 | tf_op jit(solution)/shard_map/all_gather | solution.py:626
  48.9 197.2 %all-gather.7.cloned.1.call-start = ((), (), s32[]{:S(2)}) async-start(), calls=%async_computation.2 | async-start | bytes 2621440 | tf_op jit(solution)/shard_map/all_gather | solution.py:641
  75.3 20.7 %collective-permute-start.9 = (bf16[1280,384]{1,0:T(8,128)(2,1)}, bf16[1280,384]{1,0:T(8,128)(2,1)}, u32[]{:S(2)}, u32[]{:S(2)}) collective-permute-start(bf16[1280,384]{1,0:T(8,128)(2,1)} %bitcast.220), channel_id=1, source_target_pairs={{0,16},{16,0},{1,17},{17,1},{2,18},{18,2},{3,19},{19,3},{4,20},{20... | collective-permute-start | bytes 2949128 | tf_op jit(solution)/shard_map/ppermute | solution.py:54
  123.4 16.6 %collective-permute-start.22 = (bf16[256,1024]{1,0:T(8,128)(2,1)S(1)}, bf16[256,1024]{1,0:T(8,128)(2,1)S(1)}, u32[]{:S(2)}, u32[]{:S(2)}) collective-permute-start(bf16[256,1024]{1,0:T(8,128)(2,1)S(1)} %collective-permute-done.21), channel_id=1, source_target_pairs={{0,4},{4,8},{8,12},{12,0},{1,5},{5,9},{9,13},{13,1},{2,6},{6,10},{... | collective-permute-start | bytes 1572872 | tf_op jit(solution)/shard_map/ppermute | solution.py:54
  125.3 22.6 %collective-permute-start.10 = (bf16[512,128]{1,0:T(8,128)(2,1)S(1)}, bf16[512,128]{1,0:T(8,128)(2,1)S(1)}, u32[]{:S(2)}, u32[]{:S(2)}) collective-permute-start(bf16[512,128]{1,0:T(8,128)(2,1)S(1)} %get-tuple-element.206), channel_id=1, source_target_pairs={{0,4},{4,8},{8,12},{12,0},{1,5},{5,9},{9,13},{13,1},{2,6},{6,10},{... | collective-permute-start | bytes 393224 | tf_op jit(solution)/shard_map/ppermute | solution.py:54
  125.3 22.7 %collective-permute-start.11 = (bf16[512,128]{1,0:T(8,128)(2,1)S(1)}, bf16[512,128]{1,0:T(8,128)(2,1)S(1)}, u32[]{:S(2)}, u32[]{:S(2)}) collective-permute-start(bf16[512,128]{1,0:T(8,128)(2,1)S(1)} %get-tuple-element.206), channel_id=1, source_target_pairs={{0,8},{4,12},{8,0},{12,4},{1,9},{5,13},{9,1},{13,5},{2,10},{6,14},... | collective-permute-start | bytes 393224 | tf_op jit(solution)/shard_map/ppermute | solution.py:54
  129.7 20.3 %collective-permute-start.12 = (bf16[512,128]{1,0:T(8,128)(2,1)S(1)}, bf16[512,128]{1,0:T(8,128)(2,1)S(1)}, u32[]{:S(2)}, u32[]{:S(2)}) collective-permute-start(bf16[512,128]{1,0:T(8,128)(2,1)S(1)} %get-tuple-element.206), channel_id=1, source_target_pairs={{0,12},{4,0},{8,4},{12,8},{1,13},{5,1},{9,5},{13,9},{2,14},{6,2},{... | collective-permute-start | bytes 393224 | tf_op jit(solution)/shard_map/ppermute | solution.py:54
  144.4 32.3 %collective-permute-start.23 = (bf16[1024,1024]{1,0:T(8,128)(2,1)}, bf16[1024,1024]{1,0:T(8,128)(2,1)}, u32[]{:S(2)}, u32[]{:S(2)}) collective-permute-start(bf16[1024,1024]{1,0:T(8,128)(2,1)} %bitcast.212), channel_id=1, source_target_pairs={{0,16},{16,0},{1,17},{17,1},{2,18},{18,2},{3,19},{19,3},{4,20},{20... | collective-permute-start | bytes 6291464 | tf_op jit(solution)/shard_map/ppermute | solution.py:54
  147.4 20.6 %collective-permute-start.19 = (bf16[512,1024]{1,0:T(8,128)(2,1)}, bf16[512,1024]{1,0:T(8,128)(2,1)S(1)}, u32[]{:S(2)}, u32[]{:S(2)}) collective-permute-start(bf16[512,1024]{1,0:T(8,128)(2,1)} %bitcast.216), channel_id=1, source_target_pairs={{0,16},{16,0},{1,17},{17,1},{2,18},{18,2},{3,19},{19,3},{4,20},{20... | collective-permute-start | bytes 3145736 | tf_op jit(solution)/shard_map/ppermute | solution.py:54
  162.1 19.9 %collective-permute-start.24 = (bf16[2048,128]{1,0:T(8,128)(2,1)}, bf16[2048,128]{1,0:T(8,128)(2,1)}, u32[]{:S(2)}, u32[]{:S(2)}) collective-permute-start(bf16[2048,128]{1,0:T(8,128)(2,1)} %bitcast.255), channel_id=1, source_target_pairs={{0,1},{1,0},{2,3},{3,2},{4,5},{5,4},{6,7},{7,6},{8,9},{9,8},{10,11... | collective-permute-start | bytes 1572872 | tf_op jit(solution)/shard_map/ppermute | solution.py:71
  163.7 24.0 %collective-permute-start.25 = (bf16[2048,128]{1,0:T(8,128)(2,1)}, bf16[2048,128]{1,0:T(8,128)(2,1)}, u32[]{:S(2)}, u32[]{:S(2)}) collective-permute-start(bf16[2048,128]{1,0:T(8,128)(2,1)} %bitcast.256), channel_id=1, source_target_pairs={{0,2},{2,0},{1,3},{3,1},{4,6},{6,4},{5,7},{7,5},{8,10},{10,8},{9,1... | collective-permute-start | bytes 1572872 | tf_op jit(solution)/shard_map/ppermute | solution.py:71
  164.1 23.7 %collective-permute-start.26 = (bf16[2048,128]{1,0:T(8,128)(2,1)}, bf16[2048,128]{1,0:T(8,128)(2,1)}, u32[]{:S(2)}, u32[]{:S(2)}) collective-permute-start(bf16[2048,128]{1,0:T(8,128)(2,1)} %bitcast.257), channel_id=1, source_target_pairs={{0,3},{1,2},{2,1},{3,0},{4,7},{5,6},{6,5},{7,4},{8,11},{9,10},{10,... | collective-permute-start | bytes 1572872 | tf_op jit(solution)/shard_map/ppermute | solution.py:70
  181.7 338.4 %reduce-scatter.2.cloned.1.call-start = ((), (), s32[]{:S(2)}) async-start(), calls=%async_computation.3 | async-start | bytes 19464192 | tf_op jit(solution)/shard_map/reduce_scatter | solution.py:700
  206.2 23.2 %collective-permute-start.28 = (bf16[128,2048]{1,0:T(8,128)(2,1)}, bf16[128,2048]{1,0:T(8,128)(2,1)S(1)}, u32[]{:S(2)}, u32[]{:S(2)}) collective-permute-start(bf16[128,2048]{1,0:T(8,128)(2,1)} %get-tuple-element.181), channel_id=1, source_target_pairs={{0,2},{2,0},{1,3},{3,1},{4,6},{6,4},{5,7},{7,5},{8,10},{10,8},{9,1... | collective-permute-start | bytes 1572872 | tf_op jit(solution)/shard_map/ppermute | solution.py:71
  207.6 22.6 %collective-permute-start.29 = (bf16[128,2048]{1,0:T(8,128)(2,1)}, bf16[128,2048]{1,0:T(8,128)(2,1)}, u32[]{:S(2)}, u32[]{:S(2)}) collective-permute-start(bf16[128,2048]{1,0:T(8,128)(2,1)} %get-tuple-element.180), channel_id=1, source_target_pairs={{0,3},{1,2},{2,1},{3,0},{4,7},{5,6},{6,5},{7,4},{8,11},{9,10},{10,... | collective-permute-start | bytes 1572872 | tf_op jit(solution)/shard_map/ppermute | solution.py:70
  245.7 18.4 %collective-permute-start.31 = (bf16[128,2048]{1,0:T(8,128)(2,1)}, bf16[128,2048]{1,0:T(8,128)(2,1)}, u32[]{:S(2)}, u32[]{:S(2)}) collective-permute-start(bf16[128,2048]{1,0:T(8,128)(2,1)} %collective-permute-done.30.refs_2_), channel_id=1, source_target_pairs={{0,4},{4,8},{8,12},{12,0},{1,5},{5,9},{9,13},{13,1},{2,6},{6,10},{... | collective-permute-start | bytes 1572872 | tf_op jit(solution)/shard_map/ppermute | solution.py:54
  264.1 16.9 %collective-permute-start.32 = (bf16[128,2048]{1,0:T(8,128)(2,1)}, bf16[128,2048]{1,0:T(8,128)(2,1)S(1)}, u32[]{:S(2)}, u32[]{:S(2)}) collective-permute-start(bf16[128,2048]{1,0:T(8,128)(2,1)} %collective-permute-done.31.refs_1_), channel_id=1, source_target_pairs={{0,4},{4,8},{8,12},{12,0},{1,5},{5,9},{9,13},{13,1},{2,6},{6,10},{... | collective-permute-start | bytes 1572872 | tf_op jit(solution)/shard_map/ppermute | solution.py:54
  264.8 35.1 %collective-permute-start.33 = (bf16[128,2048]{1,0:T(8,128)(2,1)}, bf16[128,2048]{1,0:T(8,128)(2,1)S(1)}, u32[]{:S(2)}, u32[]{:S(2)}) collective-permute-start(bf16[128,2048]{1,0:T(8,128)(2,1)} %get-tuple-element.127), channel_id=1, source_target_pairs={{0,4},{4,8},{8,12},{12,0},{1,5},{5,9},{9,13},{13,1},{2,6},{6,10},{... | collective-permute-start | bytes 1572872 | tf_op jit(solution)/shard_map/ppermute | solution.py:54
  318.1 16.7 %collective-permute-start.35 = (bf16[128,2048]{1,0:T(8,128)(2,1)}, bf16[128,2048]{1,0:T(8,128)(2,1)}, u32[]{:S(2)}, u32[]{:S(2)}) collective-permute-start(bf16[128,2048]{1,0:T(8,128)(2,1)} %add_convert_fusion.8), channel_id=1, source_target_pairs={{0,4},{4,8},{8,12},{12,0},{1,5},{5,9},{9,13},{13,1},{2,6},{6,10},{... | collective-permute-start | bytes 1572872 | tf_op jit(solution)/shard_map/ppermute | solution.py:54
  363.8 26.0 %collective-permute-start.39 = (bf16[1024,1024]{1,0:T(8,128)(2,1)}, bf16[1024,1024]{1,0:T(8,128)(2,1)}, u32[]{:S(2)}, u32[]{:S(2)}) collective-permute-start(bf16[1024,1024]{1,0:T(8,128)(2,1)} %convolution_convert_fusion), channel_id=1, source_target_pairs={{0,16},{16,0},{1,17},{17,1},{2,18},{18,2},{3,19},{19,3},{4,20},{20... | collective-permute-start | bytes 6291464 | tf_op jit(solution)/shard_map/ppermute | solution.py:54
  368.5 17.5 %collective-permute-start.42 = (bf16[128,2048]{1,0:T(8,128)(2,1)S(1)}, bf16[128,2048]{1,0:T(8,128)(2,1)S(1)}, u32[]{:S(2)}, u32[]{:S(2)}) collective-permute-start(bf16[128,2048]{1,0:T(8,128)(2,1)S(1)} %add_convert_fusion.6.refs_9_), channel_id=1, source_target_pairs={{0,4},{4,8},{8,12},{12,0},{1,5},{5,9},{9,13},{13,1},{2,6},{6,10},{... | collective-permute-start | bytes 1572872 | tf_op jit(solution)/shard_map/ppermute | solution.py:54
  384.3 26.1 %collective-permute-start.43 = (bf16[2048,128]{1,0:T(8,128)(2,1)S(1)}, bf16[2048,128]{1,0:T(8,128)(2,1)S(1)}, u32[]{:S(2)}, u32[]{:S(2)}) collective-permute-start(bf16[2048,128]{1,0:T(8,128)(2,1)S(1)} %get-tuple-element.185), channel_id=1, source_target_pairs={{0,1},{1,0},{2,3},{3,2},{4,5},{5,4},{6,7},{7,6},{8,9},{9,8},{10,11... | collective-permute-start | bytes 1572872 | tf_op jit(solution)/shard_map/ppermute | solution.py:71
  385.3 26.0 %collective-permute-start.44 = (bf16[2048,128]{1,0:T(8,128)(2,1)S(1)}, bf16[2048,128]{1,0:T(8,128)(2,1)S(1)}, u32[]{:S(2)}, u32[]{:S(2)}) collective-permute-start(bf16[2048,128]{1,0:T(8,128)(2,1)S(1)} %get-tuple-element.187), channel_id=1, source_target_pairs={{0,2},{2,0},{1,3},{3,1},{4,6},{6,4},{5,7},{7,5},{8,10},{10,8},{9,1... | collective-permute-start | bytes 1572872 | tf_op jit(solution)/shard_map/ppermute | solution.py:71
  385.9 41.2 %collective-permute-start.45 = (bf16[2048,128]{1,0:T(8,128)(2,1)S(1)}, bf16[2048,128]{1,0:T(8,128)(2,1)S(1)}, u32[]{:S(2)}, u32[]{:S(2)}) collective-permute-start(bf16[2048,128]{1,0:T(8,128)(2,1)S(1)} %get-tuple-element.186), channel_id=1, source_target_pairs={{0,3},{1,2},{2,1},{3,0},{4,7},{5,6},{6,5},{7,4},{8,11},{9,10},{10,... | collective-permute-start | bytes 1572872 | tf_op jit(solution)/shard_map/ppermute | solution.py:70
  394.3 36.8 %collective-permute-start.53 = (bf16[384,1024]{1,0:T(8,128)(2,1)S(1)}, bf16[384,1024]{1,0:T(8,128)(2,1)S(1)}, u32[]{:S(2)}, u32[]{:S(2)}) collective-permute-start(bf16[384,1024]{1,0:T(8,128)(2,1)S(1)} %constant_dynamic-slice_fusion.9), channel_id=1, source_target_pairs={{0,4},{4,8},{8,12},{12,0},{1,5},{5,9},{9,13},{13,1},{2,6},{6,10},{... | collective-permute-start | bytes 2359304 | tf_op jit(solution)/shard_map/ppermute | solution.py:54
  428.5 21.9 %collective-permute-start.48 = (bf16[128,1024]{1,0:T(8,128)(2,1)S(1)}, bf16[128,1024]{1,0:T(8,128)(2,1)S(1)}, u32[]{:S(2)}, u32[]{:S(2)}) collective-permute-start(bf16[128,1024]{1,0:T(8,128)(2,1)S(1)} %get-tuple-element.183), channel_id=1, source_target_pairs={{0,3},{1,2},{2,1},{3,0},{4,7},{5,6},{6,5},{7,4},{8,11},{9,10},{10,... | collective-permute-start | bytes 786440 | tf_op jit(solution)/shard_map/ppermute | solution.py:70
  431.4 27.3 %collective-permute-start.57 = (bf16[384,1024]{1,0:T(8,128)(2,1)S(1)}, bf16[384,1024]{1,0:T(8,128)(2,1)S(1)}, u32[]{:S(2)}, u32[]{:S(2)}) collective-permute-start(bf16[384,1024]{1,0:T(8,128)(2,1)S(1)} %add_convert_fusion.4), channel_id=1, source_target_pairs={{0,4},{4,8},{8,12},{12,0},{1,5},{5,9},{9,13},{13,1},{2,6},{6,10},{... | collective-permute-start | bytes 2359304 | tf_op jit(solution)/shard_map/ppermute | solution.py:54
  459.8 22.9 %collective-permute-start.58 = (bf16[384,1024]{1,0:T(8,128)(2,1)}, bf16[384,1024]{1,0:T(8,128)(2,1)}, u32[]{:S(2)}, u32[]{:S(2)}) collective-permute-start(bf16[384,1024]{1,0:T(8,128)(2,1)} %add_convert_fusion.3), channel_id=1, source_target_pairs={{0,4},{4,8},{8,12},{12,0},{1,5},{5,9},{9,13},{13,1},{2,6},{6,10},{... | collective-permute-start | bytes 2359304 | tf_op jit(solution)/shard_map/ppermute | solution.py:54
  526.4 19.3 %collective-permute-start.61 = (bf16[128,2048]{1,0:T(8,128)(2,1)S(1)}, bf16[128,2048]{1,0:T(8,128)(2,1)S(1)}, u32[]{:S(2)}, u32[]{:S(2)}) collective-permute-start(bf16[128,2048]{1,0:T(8,128)(2,1)S(1)} %get-tuple-element.176), channel_id=1, source_target_pairs={{0,1},{1,0},{2,3},{3,2},{4,5},{5,4},{6,7},{7,6},{8,9},{9,8},{10,11... | collective-permute-start | bytes 1572872 | tf_op jit(solution)/shard_map/ppermute | solution.py:71
  527.0 23.7 %collective-permute-start.62 = (bf16[128,2048]{1,0:T(8,128)(2,1)S(1)}, bf16[128,2048]{1,0:T(8,128)(2,1)S(1)}, u32[]{:S(2)}, u32[]{:S(2)}) collective-permute-start(bf16[128,2048]{1,0:T(8,128)(2,1)S(1)} %get-tuple-element.178), channel_id=1, source_target_pairs={{0,2},{2,0},{1,3},{3,1},{4,6},{6,4},{5,7},{7,5},{8,10},{10,8},{9,1... | collective-permute-start | bytes 1572872 | tf_op jit(solution)/shard_map/ppermute | solution.py:71
  528.8 23.4 %collective-permute-start.63 = (bf16[128,2048]{1,0:T(8,128)(2,1)S(1)}, bf16[128,2048]{1,0:T(8,128)(2,1)S(1)}, u32[]{:S(2)}, u32[]{:S(2)}) collective-permute-start(bf16[128,2048]{1,0:T(8,128)(2,1)S(1)} %get-tuple-element.177), channel_id=1, source_target_pairs={{0,3},{1,2},{2,1},{3,0},{4,7},{5,6},{6,5},{7,4},{8,11},{9,10},{10,... | collective-permute-start | bytes 1572872 | tf_op jit(solution)/shard_map/ppermute | solution.py:70
  (132 other events, 1383.8 us)
Sparse Core Ops, SparseCore 0:
  9.9 38.9 all-gather.8
  50.8 92.1 all-gather.4
  181.8 43.3 all-gather.6
  318.3 148.3 reduce-scatter.1
